TPU v7x, 512 devices: a whole 4x4x16 slice. The times are simulated.
512 devices in a mesh: dp: 32 (over z, core), bal: 16 (over y, x).
Axes of the slice: x: 4, y: 4, z: 16, core: 2. Of those that a mesh axis runs over, the one named last changes fastest.
Arguments:
- tiles: bfloat16 [11776, 270, 256], P(('dp', 'bal')), may hold values from -6 to 6
- cotangent: bfloat16 [11776, 32, 256], P(('dp', 'bal')), may hold values from -6 to 6
- halo_flags: int32 [11776, 3], P(('dp', 'bal')), may hold values 0 or 1
- send_plan: int32 [512, 16, 2], P(('dp', 'bal')), may hold values from -1 to 22, as said below
- spatial_weight: bfloat16 [2304, 256], P('bal'), may hold values from -0.125 to 0.125
- temporal_weight: bfloat16 [512, 256], P('bal'), may hold values from -0.25 to 0.25
Outputs:
- features: bfloat16 [11776, 32, 256], P(('dp', 'bal'))
- spatial_grad: float32 [2304, 256], P('bal', 'dp')
- temporal_grad: float32 [512, 256], P('bal', 'dp')
Inputs may be any that keep to these rules, and one draw needn't show every extreme that they name: `send_plan`: row g lists, for each worker w of owner g's bal group (bal index w, same dp index) and each pair slot q, the owner's tile slot sent there, or -1. The live slots of an owner are its slots 0 to n - 1, each named exactly once, with n from 1 to 23; in every group some owner has exactly 23. One owner sends at most 2 tiles to one worker, and some pair holds exactly 2; every worker receives exactly 12 tiles.
All inputs are finite; a program needn't handle non-finite values. No bound on the sum of `halo_flags` on one device may be relied on, other than what follows from the above.
Results may differ from a plain program's by a relative error of at most 0.0049.
Values may be sent and summed in bfloat16 or wider, within the bound.
No kernel may reach another device: no remote copies, remote signals or barrier semaphores. Data moves between devices by JAX's collectives and lax.ppermute only.
A program may use at most 128 MiB of HBM per device.

v0:
```python
import math

import jax
import jax.numpy as jnp
from jax import lax
from jax.sharding import PartitionSpec as P

TILE_ROWS = 2
TILE_COLUMNS = 4
OUTPUT_FRAMES = 4
TEMPORAL_DILATION = 2
WORK_TILES = 12
IN_FR = 6
IN_H = 5
IN_W = 9
OUT_PIX = 32


def keep_mask(halo_flag_row):
    frame_indices = jnp.arange(IN_FR)[:, None, None]
    row_ids = jnp.arange(IN_H)[None, :, None]
    col_ids = jnp.arange(IN_W)[None, None, :]
    top_ok = (row_ids > 0) | (halo_flag_row[0] > 0)
    left_ok = (col_ids > 0) | (halo_flag_row[1] > 0)
    past_frame_valid = (frame_indices >= TEMPORAL_DILATION) | (halo_flag_row[2] > 0)
    return top_ok & left_ok & past_frame_valid


def tile_pass(inputs, cotang, spatial_full, temporal_full):
    tile_number = inputs.shape[0]
    channel_index = inputs.shape[-1]
    tap_list = []
    for row_tap in range(3):
        for col_tap in range(3):
            tap_list.append(
                inputs[
                    :,
                    :,
                    row_tap : row_tap + 2 * TILE_ROWS - 1 : 2,
                    col_tap : col_tap + 2 * TILE_COLUMNS - 1 : 2,
                    :,
                ]
            )
    patches = jnp.concatenate(tap_list, axis=-1).reshape(-1, 9 * channel_index)
    pre_act = jnp.dot(patches, spatial_full, preferred_element_type=jnp.float32)
    activation = (
        jax.nn.silu(pre_act)
        .astype(jnp.bfloat16)
        .reshape(tile_number, IN_FR, TILE_ROWS * TILE_COLUMNS, channel_index)
    )
    paired_tiles = jnp.concatenate(
        [activation[:, TEMPORAL_DILATION:], activation[:, :OUTPUT_FRAMES]], axis=-1
    ).reshape(-1, 2 * channel_index)
    outputs = jnp.dot(paired_tiles, temporal_full, preferred_element_type=jnp.float32).astype(
        jnp.bfloat16
    )
    grad_out = cotang.reshape(-1, channel_index)
    grad_temp = lax.dot_general(
        paired_tiles, grad_out, (((0,), (0,)), ((), ())), preferred_element_type=jnp.float32
    )
    grad_pair = lax.dot_general(
        grad_out, temporal_full, (((1,), (1,)), ((), ())), preferred_element_type=jnp.float32
    )
    grad_pair = grad_pair.reshape(
        tile_number, OUTPUT_FRAMES, TILE_ROWS * TILE_COLUMNS, 2 * channel_index
    )
    causal_padding = jnp.zeros(
        (tile_number, TEMPORAL_DILATION, TILE_ROWS * TILE_COLUMNS, channel_index), jnp.float32
    )
    grad_activ = jnp.concatenate(
        [causal_padding, grad_pair[..., :channel_index]], axis=1
    ) + jnp.concatenate([grad_pair[..., channel_index:], causal_padding], axis=1)
    pre_view = pre_act.reshape(grad_activ.shape)
    sigmoid_v = jax.nn.sigmoid(pre_view)
    grad_pre = (
        (grad_activ * sigmoid_v * (1.0 + pre_view * (1.0 - sigmoid_v)))
        .astype(jnp.bfloat16)
        .reshape(-1, channel_index)
    )
    grad_space = lax.dot_general(
        patches, grad_pre, (((0,), (0,)), ((), ())), preferred_element_type=jnp.float32
    )
    return (outputs.reshape(tile_number, OUT_PIX, channel_index), grad_space, grad_temp)


def per_device(tiles, cotangent, halo_flags, send_plan, spatial_weight, temporal_weight):
    owned = tiles.shape[0]
    channel_index = tiles.shape[-1]
    spatial_full, temporal_full = (
        lax.all_gather(spatial_weight, "bal", axis=0, tiled=True),
        lax.all_gather(temporal_weight, "bal", axis=0, tiled=True),
    )
    shaped = tiles.reshape(owned, IN_FR, IN_H, IN_W, channel_index)
    keeping = jax.vmap(keep_mask)(halo_flags)
    masked = jnp.where(keeping[..., None], shaped, jnp.zeros_like(shaped))
    route_rows = send_plan[0]
    live_slots = jnp.any(
        route_rows.reshape(-1)[:, None] == jnp.arange(owned, dtype=jnp.int32)[None, :], axis=0
    )
    live_cot = jnp.where(live_slots[:, None, None], cotangent, jnp.zeros((), jnp.bfloat16))
    outputs, grad_space, grad_temp = tile_pass(
        masked,
        live_cot.reshape(owned, OUTPUT_FRAMES, TILE_ROWS, TILE_COLUMNS, channel_index),
        spatial_full,
        temporal_full,
    )
    features = jnp.where(live_slots[:, None, None], outputs, jnp.zeros((), jnp.bfloat16))
    data_count = lax.axis_size("dp")
    group_size = lax.axis_size("bal")
    factor = 1.0 / math.sqrt(data_count * group_size * WORK_TILES)
    part_space, part_temp = (
        lax.psum_scatter(grad_space, "dp", scatter_dimension=1, tiled=True),
        lax.psum_scatter(grad_temp, "dp", scatter_dimension=1, tiled=True),
    )
    sum_space, sum_temp = (
        lax.psum_scatter(part_space, "bal", scatter_dimension=0, tiled=True),
        lax.psum_scatter(part_temp, "bal", scatter_dimension=0, tiled=True),
    )
    return (features, sum_space * factor, sum_temp * factor)


def solution(mesh):
    in_specs = (
        P(("dp", "bal"), None, None),
        P(("dp", "bal"), None, None),
        P(("dp", "bal"), None),
        P(("dp", "bal"), None, None),
        P("bal", None),
        P("bal", None),
    )
    out_specs = (P(("dp", "bal"), None, None), P("bal", "dp"), P("bal", "dp"))
    return jax.shard_map(
        per_device, mesh=mesh, in_specs=in_specs, out_specs=out_specs, check_vma=False
    )
```

profile of v0, /device:TPU:32, one launch (start us, length us, event | category | flops | bytes accessed | tf_op | source)
XLA Modules:
  0.0 510.6 jit_solution(16662823401820421577)
XLA Ops:
  7.2 0.7 all-gather.2.cloned.1.call-update
  8.0 0.8 compare_bitcast_fusion.2
  8.8 3.0 copy.19
  11.8 0.1 broadcast_or_fusion
  11.9 0.1 broadcast_or_fusion.2
  12.0 0.1 broadcast_or_fusion.1
  12.1 1.3 broadcast_select_fusion
  13.9 4.4 copy.20
  18.3 8.8 %reshape.174 = bf16[1104,2304]{1,0:T(8,128)(2,1)} reshape(bf16[23,6,2,4,2304]{4,3,2,1,0:T(4,128)(2,1)} %copy.20) | data formatting | bytes 10174464 | tf_op jit(solution)/shard_map/reshape | solution.py:44
  27.1 0.1 copy.18
  27.2 0.1 eq.15
  27.3 24.1 %all_gather.7 = bf16[512,256]{1,0:T(8,128)(2,1)S(1)} all-gather(bf16[32,256]{1,0:T(8,128)(2,1)S(1)} %copy-done.1), channel_id=1, replica_groups=mesh['dp'=32,'bal'=16] {'bal'}, dimensions={0}, use_global_device_ids=true | all-gather | bytes 278528 | tf_op jit(solution)/shard_map/all_gather | solution.py:91
  51.4 0.1 fusion.3
  51.5 22.1 %all-gather.2.cloned.1.call-done = bf16[2304,256]{1,0:T(8,128)(2,1)} async-done(((bf16[144,256]{1,0:T(8,128)(2,1)}), bf16[2304,256]{1,0:T(8,128)(2,1)}) %all-gather.2.cloned.1.call-update) | async-done | bytes 1179664 | tf_op jit(solution)/shard_map/all_gather | solution.py:90
  73.6 4.3 multiply_convert_fusion.1
  78.0 0.4 convolution_convert_fusion
  78.4 0.5 copy-done
  78.9 0.9 broadcast_select_fusion.1
  79.7 1.2 fusion.7
  81.0 0.4 fusion
  81.5 0.2 fusion.4
  81.6 0.5 multiply_convert_fusion
  82.1 102.4 %reduce-scatter.9.cloned.1.call-done = f32[512,8]{0,1:T(8,128)} async-done(((f32[512,256]{0,1:T(8,128)}), f32[512,8]{0,1:T(8,128)}) %reduce-scatter.9.cloned.1.call-update) | async-done | bytes 16400 | tf_op jit(solution)/shard_map/reduce_scatter | solution.py:113
  184.5 1.6 copy.24
  186.2 5.6 %fusion.6 = f32[2304,256]{0,1:T(8,128)} fusion(bf16[1104,2304]{1,0:T(8,128)(2,1)} %reshape.174, bf16[1104,256]{1,0:T(8,128)(2,1)S(1)} %bitcast.40), kind=kOutput, calls=%fused_computation.36 | convolution fusion | flops 1302331392 | bytes 8011776 | tf_op jit(solution)/shard_map/dot_general | solution.py:80
  191.9 1.3 dynamic-slice
  193.8 83.7 %reduce-scatter.11.cloned.1.call-done = f32[32,8]{1,0:T(8,128)} async-done(((f32[512,8]{1,0:T(8,128)}), f32[32,8]{1,0:T(8,128)}) %reduce-scatter.11.cloned.1.call-update) | async-done | bytes 1040
  277.5 0.8 copy.25
  278.3 108.5 %reduce-scatter.7.cloned.1.call-done = f32[2304,8]{0,1:T(8,128)} async-done(((f32[2304,256]{0,1:T(8,128)}), f32[2304,8]{0,1:T(8,128)}) %reduce-scatter.7.cloned.1.call-update) | async-done | bytes 73744 | tf_op jit(solution)/shard_map/reduce_scatter | solution.py:112
  386.8 0.6 broadcast_multiply_fusion
  387.4 115.3 %all-reduce.5.cloned.1.call-done = f32[2304,8]{0,1:T(8,128)} async-done(((f32[2304,8]{0,1:T(8,128)}), f32[2304,8]{0,1:T(8,128)}) %all-reduce.5.cloned.1.call-update) | async-done | bytes 73744
  502.7 1.4 dynamic-slice_multiply_fusion
  (30 shorter events, 0.9 us)
Async XLA Ops:
  7.2 66.4 %all-gather.2.cloned.1.call-start = ((), (), s32[]{:S(2)}) async-start(), calls=%async_computation.3 | async-start | bytes 1253376 | tf_op jit(solution)/shard_map/all_gather | solution.py:90
  7.9 176.6 %reduce-scatter.9.cloned.1.call-start = ((), (), s32[]{:S(2)}) async-start(), calls=%async_computation.5 | async-start | bytes 540672 | tf_op jit(solution)/shard_map/reduce_scatter | solution.py:113
  18.3 8.8 %copy-start.2 = (s32[1,16,2]{1,2,0:T(2,128)S(1)}, s32[1,16,2]{1,2,0:T(2,128)}, u32[]{:S(2)}) copy-start(s32[1,16,2]{1,2,0:T(2,128)} %param.9) | copy-start | bytes 388
  18.3 9.0 %copy-start.1 = (bf16[32,256]{1,0:T(8,128)(2,1)S(1)}, bf16[32,256]{1,0:T(8,128)(2,1)}, u32[]{:S(2)}) copy-start(bf16[32,256]{1,0:T(8,128)(2,1)} %param.11) | copy-start | bytes 49156
  77.9 1.0 copy-start
  81.0 196.5 %reduce-scatter.11.cloned.1.call-start = ((), (), s32[]{:S(2)}) async-start(), calls=%async_computation.6 | async-start | bytes 278528
  186.1 200.6 %reduce-scatter.7.cloned.1.call-start = ((), (), s32[]{:S(2)}) async-start(), calls=%async_computation.4 | async-start | bytes 2433024 | tf_op jit(solution)/shard_map/reduce_scatter | solution.py:112
  191.8 310.9 %all-reduce.5.cloned.1.call-start = ((), (), s32[]{:S(2)}) async-start(), calls=%async_computation.7 | async-start | bytes 147456
Sparse Core Ops, SparseCore 0:
  11.0 62.5 all-gather.1
  81.1 103.3 reduce-scatter.8
  189.1 88.2 reduce-scatter.10
  280.1 106.5 reduce-scatter.6
  389.8 112.7 all-reduce.4
where the time goes:
time: 511 us
  waiting for transfers between devices  433 us (85%)
  blocking collectives  24.1 us (5%)
  local copies, waits for them, and re-layouts  21.2 us (4%)
  between operations  14.6 us (3%)
  matrix products  11.9 us (2%)
  other arithmetic  5.84 us (1%)
    unnamed x7, waiting for transfers between devices  200 us
    reduce_scatter x1, waiting for transfers between devices, per_device(): lax.psum_scatter(grad_space, 'dp', scatter_dimension=1, tiled=True)  109 us
    reduce_scatter x1, waiting for transfers between devices, per_device(): lax.psum_scatter(grad_temp, 'dp', scatter_dimension=1, tiled=True)  102 us
    all_gather x1, blocking collectives, per_device(): lax.all_gather(temporal_weight, 'bal', axis=0, tiled=True)  24.1 us
    all_gather x1, waiting for transfers between devices, per_device(): lax.all_gather(spatial_weight, 'bal', axis=0, tiled=True)  22.1 us
  transfers between devices with their start and end apart: 5, of which 5 were waited for; matrix products, arithmetic and copies ran while one was open for 6% of the time, Pallas kernels for 0%

commit v1 on v0

v1 whole, which is shorter than its diff:
```python
import functools
import math

import jax
import jax.numpy as jnp
from jax import lax
from jax.experimental import pallas as pl
from jax.experimental.pallas import tpu as pltpu
from jax.sharding import PartitionSpec as P

C = 256
OWNED = 23
IN_PIX = 270
OUT_PIX = 32
ACT_PIX = 48
TAPS = 9
WORK_TILES = 12
GROUP = 8
STEPS = 3
PAD_TILES = GROUP * STEPS
ROWS = PAD_TILES * ACT_PIX
GROUP_ROWS = GROUP * ACT_PIX
COT_ROWS = PAD_TILES * OUT_PIX
GROUP_COT = GROUP * OUT_PIX
WINDOWS = ((0, 128), (80, 128), (160, 110))
PAIR_ROWS = 16 * TAPS
BF = jnp.bfloat16
F32 = jnp.float32


def selection():
    row = lax.broadcasted_iota(jnp.int32, (3, PAIR_ROWS, 128), 1)
    col = lax.broadcasted_iota(jnp.int32, (3, PAIR_ROWS, 128), 2)
    group = lax.broadcasted_iota(jnp.int32, (3, PAIR_ROWS, 128), 0)
    tap, cell = row // 16, row % 16
    frame, i, j = cell // 8, (cell // 4) % 2, cell % 4
    source = (2 * group + frame) * 45 + (2 * i + tap // 3) * 9 + 2 * j + tap % 3
    pick = (source == col + 80 * group).astype(BF)
    kind = lax.broadcasted_iota(jnp.int32, (3, 8, 128), 1)
    cell = lax.broadcasted_iota(jnp.int32, (3, 8, 128), 2) + 80 * lax.broadcasted_iota(
        jnp.int32, (3, 8, 128), 0
    )
    top = (kind == 0) & (cell % 45 < 9)
    left = (kind == 1) & (cell % 9 == 0)
    past = (kind == 2) & (cell < 90)
    return pick, (top | left | past).astype(F32)


def live_count(plan_ref):
    count = plan_ref[0, 0]
    for q in range(2):
        for w in range(16):
            count = jnp.maximum(count, plan_ref[q, w])
    return count + 1


def patch_kernel(flags_ref, plan_ref, tiles_ref, cot_ref, pick_ref, mark_ref, perm_ref,
                 patch_ref, patcht_ref, cotl_ref, cotp_ref):
    step = pl.program_id(0)
    count = live_count(plan_ref)
    for t in range(GROUP):
        slot = step * GROUP + t
        rows = slice(t * ACT_PIX, (t + 1) * ACT_PIX)

        @pl.when(slot < OWNED)
        def _():
            flag = jnp.minimum(slot, OWNED - 1)
            off = [jnp.where(flags_ref[k, flag] > 0, 0.0, 1.0) for k in range(3)]
            for g, (first, size) in enumerate(WINDOWS):
                marks = mark_ref[g]
                out = marks[0:1] * off[0] + marks[1:2] * off[1] + marks[2:3] * off[2]
                keep = jnp.where(out > 0.0, 0.0, 1.0).astype(BF)
                chosen = (pick_ref[g] * keep)[:, :size]
                got = jnp.dot(chosen, tiles_ref[t, first:first + size, :],
                              preferred_element_type=F32).astype(BF)
                for tap in range(TAPS):
                    patch_ref[t * ACT_PIX + 16 * g:t * ACT_PIX + 16 * (g + 1),
                              tap * C:(tap + 1) * C] = got[tap * 16:(tap + 1) * 16]

        @pl.when(slot >= OWNED)
        def _():
            patch_ref[rows, :] = jnp.zeros((ACT_PIX, TAPS * C), BF)

        cells = slice(t * OUT_PIX, (t + 1) * OUT_PIX)
        cot = jnp.where(slot < count, cot_ref[t].astype(F32), 0.0).astype(BF)
        cotl_ref[cells, :] = cot
        cotp_ref[cells, :] = jnp.dot(cot, perm_ref[...], preferred_element_type=F32).astype(BF)
    for tap in range(TAPS):
        patcht_ref[tap * C:(tap + 1) * C, :] = patch_ref[:, tap * C:(tap + 1) * C].T


def main_kernel(plan_ref, weights_ref, cotl_ref, cotp_ref, perm_ref, patch_hbm, patcht_hbm,
                feat_ref, keep_ref, send_ref,
                patch_s, patcht_s, spatial_s, temporal_s, pair_s, gpre_s, sems):
    copies = [
        pltpu.make_async_copy(patch_hbm.at[pl.ds(g * GROUP_ROWS, GROUP_ROWS), :],
                              patch_s.at[pl.ds(g * GROUP_ROWS, GROUP_ROWS), :], sems.at[g])
        for g in range(STEPS)
    ]
    copies.append(pltpu.make_async_copy(patcht_hbm, patcht_s, sems.at[STEPS]))
    for copy in copies:
        copy.start()
    count = live_count(plan_ref)
    for b in range(16):
        spatial_s[b * 144:(b + 1) * 144, :] = weights_ref[b, :144, :]
        temporal_s[b * 32:(b + 1) * 32, :] = weights_ref[b, 144:, :]
    for g in range(STEPS):
        copies[g].wait()
        rows = slice(g * GROUP_ROWS, (g + 1) * GROUP_ROWS)
        cells = slice(g * GROUP_COT, (g + 1) * GROUP_COT)
        pre = jnp.dot(patch_s[rows, :], spatial_s[...], preferred_element_type=F32)
        sig = 1.0 / (1.0 + jnp.exp(-pre))
        act = (pre * sig).astype(BF)
        slope = sig * (1.0 + pre * (1.0 - sig))
        for t in range(GROUP):
            out = slice(g * GROUP_COT + t * OUT_PIX, g * GROUP_COT + (t + 1) * OUT_PIX)
            pair_s[out, :C] = act[t * ACT_PIX + 16:(t + 1) * ACT_PIX]
            pair_s[out, C:] = act[t * ACT_PIX:t * ACT_PIX + OUT_PIX]
        gpair = lax.dot_general(cotl_ref[cells, :], temporal_s[...], (((1,), (1,)), ((), ())),
                                preferred_element_type=F32)
        pieces = []
        for t in range(GROUP):
            a, b, c = t * OUT_PIX, t * OUT_PIX + 16, (t + 1) * OUT_PIX
            pieces.append(gpair[a:b, C:])
            pieces.append(gpair[a:b, :C] + gpair[b:c, C:])
            pieces.append(gpair[b:c, :C])
        gact = jnp.concatenate(pieces, axis=0)
        gpre = (gact * slope).astype(BF)
        gpre_s[rows, :] = jnp.dot(gpre, perm_ref[...], preferred_element_type=F32).astype(BF)
        feat = jnp.dot(pair_s[cells, :], temporal_s[...], preferred_element_type=F32).astype(BF)
        for t in range(GROUP):
            slot = g * GROUP + t
            if slot < OWNED:
                one = feat[t * OUT_PIX:(t + 1) * OUT_PIX]
                feat_ref[slot] = jnp.where(slot < count, one, jnp.zeros_like(one))

    def put(first, grad):
        last = first + grad.shape[0]
        for b in range(first // 144, (last - 1) // 144 + 1):
            lo, hi = max(first, 144 * b), min(last, 144 * (b + 1))
            piece = grad[lo - first:hi - first]
            keep_ref[b, lo - 144 * b:hi - 144 * b, :] = piece[:, :128]
            send_ref[b, lo - 144 * b:hi - 144 * b, :] = piece[:, 128:].astype(BF)

    temporal = lax.dot_general(pair_s[...], cotp_ref[...], (((0,), (0,)), ((), ())),
                               preferred_element_type=F32)
    for b in range(16):
        piece = temporal[b * 32:(b + 1) * 32]
        keep_ref[b, 144:, :] = piece[:, :128]
        send_ref[b, 144:, :] = piece[:, 128:].astype(BF)
    copies[STEPS].wait()
    for tap in range(TAPS):
        put(tap * C, jnp.dot(patcht_s[tap * C:(tap + 1) * C, :], gpre_s[...],
                             preferred_element_type=F32))


def per_device(tiles, cotangent, halo_flags, send_plan, spatial_weight, temporal_weight):
    core = lax.axis_index("dp") % 2
    mine = jnp.concatenate([spatial_weight, temporal_weight], axis=0)
    blocks = jnp.broadcast_to(mine[None], (16,) + mine.shape)
    weights = lax.all_to_all(blocks, "bal", 0, 0)

    pick, marks = selection()
    row = lax.broadcasted_iota(jnp.int32, (C, C), 0)
    col = lax.broadcasted_iota(jnp.int32, (C, C), 1)
    wanted = ((col % 128) // 8) * 16 + jnp.bitwise_xor(core, col // 128) * 8 + col % 8
    perm = (row == wanted).astype(BF)
    flags = halo_flags.T
    plan = send_plan[0].T

    whole = lambda shape: pl.BlockSpec(shape, lambda s: (0,) * len(shape))
    smem = pl.BlockSpec(memory_space=pltpu.SMEM)
    patches, patches_t, cot_live, cot_perm = pl.pallas_call(
        patch_kernel,
        grid=(STEPS,),
        in_specs=[
            smem, smem,
            pl.BlockSpec((GROUP, IN_PIX, C), lambda s: (s, 0, 0)),
            pl.BlockSpec((GROUP, OUT_PIX, C), lambda s: (s, 0, 0)),
            whole((3, PAIR_ROWS, 128)), whole((3, 8, 128)), whole((C, C)),
        ],
        out_specs=[
            pl.BlockSpec((GROUP_ROWS, TAPS * C), lambda s: (s, 0)),
            pl.BlockSpec((TAPS * C, GROUP_ROWS), lambda s: (0, s)),
            pl.BlockSpec((GROUP_COT, C), lambda s: (s, 0)),
            pl.BlockSpec((GROUP_COT, C), lambda s: (s, 0)),
        ],
        out_shape=[
            jax.ShapeDtypeStruct((ROWS, TAPS * C), BF),
            jax.ShapeDtypeStruct((TAPS * C, ROWS), BF),
            jax.ShapeDtypeStruct((COT_ROWS, C), BF),
            jax.ShapeDtypeStruct((COT_ROWS, C), BF),
        ],
        compiler_params=pltpu.CompilerParams(vmem_limit_bytes=40 * 2**20),
        cost_estimate=pl.CostEstimate(flops=6 * 10**9, bytes_accessed=15 * 10**6, transcendentals=0),
        name="patches",
    )(flags, plan, tiles, cotangent, pick, marks, perm)

    vmem = pl.BlockSpec(memory_space=pltpu.VMEM)
    hbm = pl.BlockSpec(memory_space=pl.ANY)
    features, keep, send = pl.pallas_call(
        main_kernel,
        in_specs=[smem, vmem, vmem, vmem, vmem, hbm, hbm],
        out_specs=[vmem, vmem, vmem],
        out_shape=[
            jax.ShapeDtypeStruct((OWNED, OUT_PIX, C), BF),
            jax.ShapeDtypeStruct((16, 176, 128), F32),
            jax.ShapeDtypeStruct((16, 176, 128), BF),
        ],
        scratch_shapes=[
            pltpu.VMEM((ROWS, TAPS * C), BF),
            pltpu.VMEM((TAPS * C, ROWS), BF),
            pltpu.VMEM((TAPS * C, C), BF),
            pltpu.VMEM((2 * C, C), BF),
            pltpu.VMEM((COT_ROWS, 2 * C), BF),
            pltpu.VMEM((ROWS, C), BF),
            pltpu.SemaphoreType.DMA((STEPS + 1,)),
        ],
        compiler_params=pltpu.CompilerParams(vmem_limit_bytes=48 * 2**20),
        cost_estimate=pl.CostEstimate(flops=4 * 10**9, bytes_accessed=15 * 10**6, transcendentals=0),
        name="section",
    )(plan, weights, cot_live, cot_perm, perm, patches, patches_t)

    other = lax.ppermute(send, "dp", [(i, i ^ 1) for i in range(32)])
    chip = (keep + other.astype(F32)).astype(BF)
    part = lax.all_to_all(chip, "bal", 0, 0)
    part = jnp.sum(part.astype(F32), axis=0)
    part = part.T.reshape(16, 8, 176)
    along_z = [[2 * z + c for z in range(16)] for c in range(2)]
    last = lax.all_to_all(part, "dp", 0, 0, axis_index_groups=along_z)
    factor = 1.0 / math.sqrt(lax.axis_size("dp") * lax.axis_size("bal") * WORK_TILES)
    total = jnp.sum(last, axis=0) * factor
    return features, total[:, :144].T, total[:, 144:].T


def solution(mesh):
    in_specs = (
        P(("dp", "bal"), None, None),
        P(("dp", "bal"), None, None),
        P(("dp", "bal"), None),
        P(("dp", "bal"), None, None),
        P("bal", None),
        P("bal", None),
    )
    out_specs = (P(("dp", "bal"), None, None), P("bal", "dp"), P("bal", "dp"))
    return jax.shard_map(
        per_device, mesh=mesh, in_specs=in_specs, out_specs=out_specs, check_vma=False
    )
```

time: 511 us -> 92.4 us (0.18)
  waiting for transfers between devices: 433 us -> 8.42 us
  blocking collectives: 24.1 us -> 45.2 us
  Pallas kernels: 0 us -> 19.9 us
  local copies, waits for them, and re-layouts: 21.2 us -> 6.87 us
  between operations: 14.6 us -> 0.82 us
  matrix products: 11.9 us -> 0 us
  starting transfers between devices: 0.2 us -> 9.09 us
    reduce_scatter x2 -> x0, waiting for transfers between devices: 211 us -> none  [the longest x1 109 us: per_device(): lax.psum_scatter(grad_space, 'dp', scatter_dimension=1, tiled=True)]
    unnamed x7 -> x0, waiting for transfers between devices: 200 us -> none
    all_to_all x0 -> x2, blocking collectives: none -> 45.2 us  [the longest x1 28.3 us: per_device(): last = lax.all_to_all(part, 'dp', 0, 0, axis_index_groups=along_z)]
    all_gather x1 -> x0, blocking collectives: 24.1 us -> none  [per_device(): lax.all_gather(temporal_weight, 'bal', axis=0, tiled=True)]
    all_gather x1 -> x0, waiting for transfers between devices: 22.1 us -> none  [per_device(): lax.all_gather(spatial_weight, 'bal', axis=0, tiled=True)]
    pallas_call x0 -> x2, Pallas kernels: none -> 19.9 us  [the longest x1 11.5 us: per_device(): pl.pallas_call(patch_kernel, grid=(STEPS,), in_specs=[smem, smem, pl.Bloc...]
    dot_general x5 -> x0, matrix products: 11.9 us -> none  [the longest x1 5.59 us: tile_pass(): lax.dot_general(patches, grad_pre, (((0,), (0,)), ((), ())), preferred_el...]
    reshape x1 -> x0, local copies, waits for them, and re-layouts: 8.84 us -> none  [tile_pass(): patches = jnp.concatenate(tap_list, axis=-1).reshape(-1, 9 * channel_index)]
  transfers between devices with their start and end apart: 5 -> 2, of which waited for: 5 -> 2; matrix products, arithmetic and copies ran while one was open for 6% -> 1% of each run, Pallas kernels for 0% -> 13%
where the time goes in v1:
time: 92.4 us; the launch traced here: 92 us
  blocking collectives  45.2 us (49%)
  Pallas kernels  19.9 us (22%)
  starting transfers between devices  9.09 us (10%)
  waiting for transfers between devices  8.42 us (9%)
  local copies, waits for them, and re-layouts  6.87 us (7%)
  other arithmetic  1.74 us (2%)
    all_to_all x1, blocking collectives, per_device(): last = lax.all_to_all(part, 'dp', 0, 0, axis_index_groups=along_z)  28.3 us
    all_to_all x1, blocking collectives, per_device(): part = lax.all_to_all(chip, 'bal', 0, 0)  16.8 us
    pallas_call x1, Pallas kernels, per_device(): pl.pallas_call(patch_kernel, grid=(STEPS,), in_specs=[smem, smem, pl.Bloc...  11.5 us
    pallas_call x1, Pallas kernels, per_device(): pl.pallas_call(main_kernel, in_specs=[smem, vmem, vmem, vmem, vmem, hbm,...  8.41 us
    all_to_all x1, starting transfers between devices, per_device(): weights = lax.all_to_all(blocks, 'bal', 0, 0)  7.17 us
    all_to_all x1, waiting for transfers between devices, per_device(): weights = lax.all_to_all(blocks, 'bal', 0, 0)  6.26 us
    unnamed x10, local copies, waits for them, and re-layouts  4.3 us
    ppermute x1, waiting for transfers between devices, per_device(): other = lax.ppermute(send, 'dp', [(i, i ^ 1) for i in range(32)])  2.16 us
  transfers between devices with their start and end apart: 2, of which 2 were waited for; matrix products, arithmetic and copies ran while one was open for 1% of the time, Pallas kernels for 13%

profile of v1, /device:TPU:32, one launch (start us, length us, event | category | flops | bytes accessed | tf_op | source)
XLA Modules:
  0.0 92.0 jit_solution(17363905725707423495)
XLA Ops:
  0.6 0.9 pad_maximum_fusion
  1.5 1.2 %broadcast_in_dim.2 = bf16[16,176,256]{2,1,0:T(8,128)(2,1)} broadcast(bf16[176,256]{1,0:T(8,128)(2,1)S(1)} %pad_maximum_fusion), dimensions={1,2} | broadcast | bytes 1531904 | tf_op jit(solution)/shard_map/broadcast_in_dim | solution.py:160
  2.8 0.0 copy-start.1
  2.8 0.0 copy-start.2
  2.8 0.0 copy-start.3
  2.8 7.2 %all-to-all-start = ((bf16[16,176,256]{2,1,0:T(8,128)(2,1)}), bf16[16,176,256]{2,1,0:T(8,128)(2,1)S(1)}, u32[]{:S(2)}, u32[]{:S(2)}) async-start(bf16[16,176,256]{2,1,0:T(8,128)(2,1)} %broadcast_in_dim.2), calls=%async_computation | async-start | bytes 2883584 | tf_op jit(solution)/shard_map/all_to_all | solution.py:161
  10.1 0.1 fusion.49.mark_ref
  10.2 0.3 fusion.35.pick_ref
  10.6 0.0 copy-done.1
  10.6 0.0 copy-done.2
  10.6 0.0 copy-done.3
  10.6 0.0 copy-start
  10.6 1.9 %copy-done = bf16[23,270,256]{2,1,0:T(8,128)(2,1)S(1)} copy-done((bf16[23,270,256]{2,1,0:T(8,128)(2,1)S(1)}, bf16[23,270,256]{2,1,0:T(8,128)(2,1)}, u32[]{:S(2)}) %copy-start) | copy-done | bytes 3179544
  12.5 11.5 %patches.1 = (bf16[1152,2304]{1,0:T(8,128)(2,1)S(1)}, bf16[2304,1152]{1,0:T(8,128)(2,1)}, bf16[768,256]{1,0:T(8,128)(2,1)S(1)}, bf16[768,256]{1,0:T(8,128)(2,1)S(1)}) custom-call(s32[3,23]{1,0:T(4,128)S(1)} %bitcast.10, s32[2,16]{1,0:T(2,128)S(1)} %bitcast.11, bf16[23,270,256]{2,1,0:T(8,128)(2,1)S(1)} %copy-done, bf16[23,32,256]{2,1,0:T(8,128)(2,1)S(1)} %copy-done.1, ...), custom_call_target="tpu_custom_call" | custom-call | flops 6000000000 | bytes 15000000 | tf_op jit(solution)/shard_map/patches/pallas_call | solution.py:173
  24.0 0.0 copy-start.4
  24.0 2.4 %copy-done.4 = bf16[1152,2304]{1,0:T(8,128)(2,1)} copy-done((bf16[1152,2304]{1,0:T(8,128)(2,1)}, bf16[1152,2304]{1,0:T(8,128)(2,1)S(1)}, u32[]{:S(2)}) %copy-start.4) | copy-done | bytes 5308440
  26.4 6.3 %all-to-all-done.weights_ref = bf16[16,176,256]{2,1,0:T(8,128)(2,1)S(1)} async-done(((bf16[16,176,256]{2,1,0:T(8,128)(2,1)}), bf16[16,176,256]{2,1,0:T(8,128)(2,1)S(1)}, u32[]{:S(2)}, u32[]{:S(2)}) %all-to-all-start) | async-done | bytes 1441824 | tf_op jit(solution)/shard_map/all_to_all | solution.py:161
  32.7 8.4 %section.1 = (bf16[23,32,256]{2,1,0:T(8,128)(2,1)}, f32[16,176,128]{2,1,0:T(8,128)S(1)}, bf16[16,176,128]{2,1,0:T(8,128)(2,1)S(1)}) custom-call(s32[2,16]{1,0:T(2,128)S(1)} %bitcast.12, bf16[16,176,256]{2,1,0:T(8,128)(2,1)S(1)} %all-to-all-done.weights_ref, bf16[768,256]{1,0:T(8,128)(2,1)S(1)} %get-tuple-element.10.cotl_ref, ...), custom_call_target="tpu_custom_call" | custom-call | flops 4000000000 | bytes 15000000 | tf_op jit(solution)/shard_map/section/pallas_call | solution.py:201
  41.1 1.9 %collective-permute-start = (bf16[16,176,128]{2,1,0:T(8,128)(2,1)S(1)}, bf16[16,176,128]{2,1,0:T(8,128)(2,1)S(1)}, u32[]{:S(2)}, u32[]{:S(2)}) collective-permute-start(bf16[16,176,128]{2,1,0:T(8,128)(2,1)S(1)} %get-tuple-element.16), channel_id=1, source_target_pairs={{0,16},{16,0},{32,48},{48,32},{64,80},{80,64},{96,112},{112,96},{1... | collective-permute-start | bytes 2162696 | tf_op jit(solution)/shard_map/ppermute | solution.py:224
  43.0 2.2 %collective-permute-done = bf16[16,176,128]{2,1,0:T(8,128)(2,1)S(1)} collective-permute-done((bf16[16,176,128]{2,1,0:T(8,128)(2,1)S(1)}, bf16[16,176,128]{2,1,0:T(8,128)(2,1)S(1)}, u32[]{:S(2)}, u32[]{:S(2)}) %collective-permute-start) | collective-permute-done | bytes 720928 | tf_op jit(solution)/shard_map/ppermute | solution.py:224
  45.2 0.2 add_convert_fusion
  45.3 16.8 %all_to_all.15 = bf16[16,176,128]{2,1,0:T(8,128)(2,1)S(1)} all-to-all(bf16[16,176,128]{2,1,0:T(8,128)(2,1)S(1)} %add_convert_fusion), channel_id=1, replica_groups=mesh['dp'=32,'bal'=16] {'bal'}, dimensions={0} | all-to-all | bytes 1441792 | tf_op jit(solution)/shard_map/all_to_all | solution.py:226
  62.2 0.1 convert_reduce_fusion
  62.3 0.1 copy.9
  62.4 28.3 %all_to_all.16 = f32[16,8,176]{2,1,0:T(8,128)S(1)} all-to-all(f32[16,8,176]{2,1,0:T(8,128)S(1)} %bitcast.13), channel_id=1, replica_groups={{0,32,64,96,128,160,192,224,256,288,320,352,384,416,448,480},{16,48,80,..., dimensions={0} | all-to-all | bytes 180224 | tf_op jit(solution)/shard_map/all_to_all | solution.py:230
  90.7 0.7 slice_bitcast_fusion.1
  91.4 0.6 slice_bitcast_fusion
  (14 shorter events, 0.1 us)
Async XLA Ops:
  2.8 7.8 %copy-start.1 = (bf16[23,32,256]{2,1,0:T(8,128)(2,1)S(1)}, bf16[23,32,256]{2,1,0:T(8,128)(2,1)}, u32[]{:S(2)}) copy-start(bf16[23,32,256]{2,1,0:T(8,128)(2,1)} %cot_ref.1) | copy-start | bytes 1130500
  2.8 7.8 %copy-start.2 = (s32[23,3]{0,1:T(4,128)S(1)}, s32[23,3]{0,1:T(4,128)}, u32[]{:S(2)}) copy-start(s32[23,3]{0,1:T(4,128)} %param.8) | copy-start | bytes 832
  2.8 7.8 %copy-start.3 = (s32[1,16,2]{1,2,0:T(2,128)S(1)}, s32[1,16,2]{1,2,0:T(2,128)}, u32[]{:S(2)}) copy-start(s32[1,16,2]{1,2,0:T(2,128)} %param.9) | copy-start | bytes 388
  2.8 29.9 %all-to-all-start = ((bf16[16,176,256]{2,1,0:T(8,128)(2,1)}), bf16[16,176,256]{2,1,0:T(8,128)(2,1)S(1)}, u32[]{:S(2)}, u32[]{:S(2)}) async-start(bf16[16,176,256]{2,1,0:T(8,128)(2,1)} %broadcast_in_dim.2), calls=%async_computation | async-start | bytes 2883584 | tf_op jit(solution)/shard_map/all_to_all | solution.py:161
  10.6 1.9 %copy-start = (bf16[23,270,256]{2,1,0:T(8,128)(2,1)S(1)}, bf16[23,270,256]{2,1,0:T(8,128)(2,1)}, u32[]{:S(2)}) copy-start(bf16[23,270,256]{2,1,0:T(8,128)(2,1)} %tiles_ref.1) | copy-start | bytes 9538564
  24.0 2.4 %copy-start.4 = (bf16[1152,2304]{1,0:T(8,128)(2,1)}, bf16[1152,2304]{1,0:T(8,128)(2,1)S(1)}, u32[]{:S(2)}) copy-start(bf16[1152,2304]{1,0:T(8,128)(2,1)S(1)} %get-tuple-element.12.patch_hbm) | copy-start | bytes 15925252
  41.1 4.1 %collective-permute-start = (bf16[16,176,128]{2,1,0:T(8,128)(2,1)S(1)}, bf16[16,176,128]{2,1,0:T(8,128)(2,1)S(1)}, u32[]{:S(2)}, u32[]{:S(2)}) collective-permute-start(bf16[16,176,128]{2,1,0:T(8,128)(2,1)S(1)} %get-tuple-element.16), channel_id=1, source_target_pairs={{0,16},{16,0},{32,48},{48,32},{64,80},{80,64},{96,112},{112,96},{1... | collective-permute-start | bytes 2162696 | tf_op jit(solution)/shard_map/ppermute | solution.py:224

commit v2 on v1

v2 whole, which is shorter than its diff:
```python
import functools
import math

import jax
import jax.numpy as jnp
from jax import lax
from jax.experimental import pallas as pl
from jax.experimental.pallas import tpu as pltpu
from jax.sharding import PartitionSpec as P

C = 256
OWNED = 23
IN_PIX = 270
OUT_PIX = 32
ACT_PIX = 48
TAPS = 9
WORK_TILES = 12
FACTOR = 1.0 / math.sqrt(512 * WORK_TILES)
GROUP = 8
STEPS = 3
PAD_TILES = GROUP * STEPS
ROWS = PAD_TILES * ACT_PIX
GROUP_ROWS = GROUP * ACT_PIX
DOT_ROWS = 192
COT_ROWS = PAD_TILES * OUT_PIX
GROUP_COT = GROUP * OUT_PIX
WINDOWS = ((0, 128), (80, 128), (160, 110))
PAIR_ROWS = 16 * TAPS
SHARE = 96
BF = jnp.bfloat16
F32 = jnp.float32


def selection():
    row = lax.broadcasted_iota(jnp.int32, (3, PAIR_ROWS, 128), 1)
    col = lax.broadcasted_iota(jnp.int32, (3, PAIR_ROWS, 128), 2)
    group = lax.broadcasted_iota(jnp.int32, (3, PAIR_ROWS, 128), 0)
    tap, cell = row // 16, row % 16
    frame, i, j = cell // 8, (cell // 4) % 2, cell % 4
    source = (2 * group + frame) * 45 + (2 * i + tap // 3) * 9 + 2 * j + tap % 3
    pick = (source == col + 80 * group).astype(BF)
    kind = lax.broadcasted_iota(jnp.int32, (3, 8, 128), 1)
    cell = lax.broadcasted_iota(jnp.int32, (3, 8, 128), 2) + 80 * lax.broadcasted_iota(
        jnp.int32, (3, 8, 128), 0
    )
    top = (kind == 0) & (cell % 45 < 9)
    left = (kind == 1) & (cell % 9 == 0)
    past = (kind == 2) & (cell < 90)
    return pick, (top | left | past).astype(F32)


def live_count(plan_ref):
    count = plan_ref[0, 0]
    for q in range(2):
        for w in range(16):
            count = jnp.maximum(count, plan_ref[q, w])
    return count + 1


def patch_kernel(flags_ref, plan_ref, tiles_hbm, cot_ref, pick_ref, mark_ref, perm_ref,
                 patch_hbm, patcht_hbm, cotl_ref, cotp_ref,
                 tiles_s, patch_ref, patcht_ref, sems, out_sems):
    copies = []
    for g in range(STEPS):
        first, last = g * GROUP, min((g + 1) * GROUP, OWNED)
        span = pl.ds(first, last - first)
        copies.append(pltpu.make_async_copy(tiles_hbm.at[span], tiles_s.at[span], sems.at[g]))
        copies[g].start()
    count = live_count(plan_ref)
    for slot in range(OWNED):
        cells = slice(slot * OUT_PIX, (slot + 1) * OUT_PIX)
        one = cot_ref[slot]
        cotl_ref[cells, :] = jnp.where(slot < count, one, jnp.zeros_like(one))
    cotl_ref[OWNED * OUT_PIX:, :] = jnp.zeros((OUT_PIX, C), BF)
    cotp_ref[...] = jnp.dot(cotl_ref[...], perm_ref[...], preferred_element_type=F32).astype(BF)
    writes = []
    for g in range(STEPS):
        copies[g].wait()
        for slot in range(g * GROUP, min((g + 1) * GROUP, OWNED)):
            off = [jnp.where(flags_ref[k, slot] > 0, 0.0, 1.0) for k in range(3)]
            for w, (first, size) in enumerate(WINDOWS):
                marks = mark_ref[w]
                out = marks[0:1] * off[0] + marks[1:2] * off[1] + marks[2:3] * off[2]
                keep = jnp.where(out > 0.0, 0.0, 1.0).astype(BF)
                chosen = (pick_ref[w] * keep)[:, :size]
                got = jnp.dot(chosen, tiles_s[slot, first:first + size, :],
                              preferred_element_type=F32).astype(BF)
                row = slot * ACT_PIX + 16 * w
                for tap in range(TAPS):
                    patch_ref[row:row + 16, tap * C:(tap + 1) * C] = got[tap * 16:(tap + 1) * 16]
        if g == STEPS - 1:
            patch_ref[OWNED * ACT_PIX:, :] = jnp.zeros((ACT_PIX, TAPS * C), BF)
        rows = slice(g * GROUP_ROWS, (g + 1) * GROUP_ROWS)
        for tap in range(TAPS):
            patcht_ref[tap * C:(tap + 1) * C, rows] = patch_ref[rows, tap * C:(tap + 1) * C].T
        span = pl.ds(g * GROUP_ROWS, GROUP_ROWS)
        writes.append(pltpu.make_async_copy(patch_ref.at[span, :], patch_hbm.at[span, :],
                                            out_sems.at[2 * g]))
        writes.append(pltpu.make_async_copy(patcht_ref.at[:, span], patcht_hbm.at[:, span],
                                            out_sems.at[2 * g + 1]))
        writes[2 * g].start()
        writes[2 * g + 1].start()
    for write in writes:
        write.wait()


def main_kernel(core_ref, plan_ref, got_ref, other_ref, cotl_ref, cotp_ref, perm_ref,
                patch_hbm, patcht_hbm, feat_ref, keep_ref, send_ref,
                patch_s, patcht_s, spatial_s, temporal_s, pair_s, gpre_s, sems):
    spans = [pl.ds(g * GROUP_ROWS, GROUP_ROWS) for g in range(STEPS)]
    copies = [pltpu.make_async_copy(patch_hbm.at[span, :], patch_s.at[span, :], sems.at[g])
              for g, span in enumerate(spans)]
    copies.append(pltpu.make_async_copy(patcht_hbm, patcht_s, sems.at[STEPS]))
    for copy in copies:
        copy.start()
    count = live_count(plan_ref)

    def place(low_ref, high_ref):
        for b in range(16):
            spatial_s[b * 144:b * 144 + SHARE, :] = low_ref[b]
            spatial_s[b * 144 + SHARE:(b + 1) * 144, :] = high_ref[b, 2 * SHARE - 176:SHARE - 32, :]
            temporal_s[b * 32:(b + 1) * 32, :] = high_ref[b, SHARE - 32:, :]

    @pl.when(core_ref[0] == 0)
    def _():
        place(got_ref, other_ref)

    @pl.when(core_ref[0] != 0)
    def _():
        place(other_ref, got_ref)

    for g in range(STEPS):
        copies[g].wait()
        rows = slice(g * GROUP_ROWS, (g + 1) * GROUP_ROWS)
        cells = slice(g * GROUP_COT, (g + 1) * GROUP_COT)
        pre = jnp.concatenate([
            jnp.dot(patch_s[r:r + DOT_ROWS, :], spatial_s[...], preferred_element_type=F32)
            for r in range(g * GROUP_ROWS, (g + 1) * GROUP_ROWS, DOT_ROWS)
        ], axis=0)
        sig = 1.0 / (1.0 + jnp.exp(-pre))
        act = (pre * sig).astype(BF)
        slope = sig * (1.0 + pre * (1.0 - sig))
        for t in range(GROUP):
            out = slice(g * GROUP_COT + t * OUT_PIX, g * GROUP_COT + (t + 1) * OUT_PIX)
            pair_s[out, :C] = act[t * ACT_PIX + 16:(t + 1) * ACT_PIX]
            pair_s[out, C:] = act[t * ACT_PIX:t * ACT_PIX + OUT_PIX]
        gpair = lax.dot_general(cotl_ref[cells, :], temporal_s[...], (((1,), (1,)), ((), ())),
                                preferred_element_type=F32)
        pieces = []
        for t in range(GROUP):
            a, b, c = t * OUT_PIX, t * OUT_PIX + 16, (t + 1) * OUT_PIX
            pieces.append(gpair[a:b, C:])
            pieces.append(gpair[a:b, :C] + gpair[b:c, C:])
            pieces.append(gpair[b:c, :C])
        gact = jnp.concatenate(pieces, axis=0)
        gpre = (gact * slope).astype(BF)
        gpre_s[rows, :] = jnp.dot(gpre, perm_ref[...], preferred_element_type=F32).astype(BF)
        feat = jnp.dot(pair_s[cells, :], temporal_s[...], preferred_element_type=F32).astype(BF)
        for t in range(GROUP):
            slot = g * GROUP + t
            if slot < OWNED:
                one = feat[t * OUT_PIX:(t + 1) * OUT_PIX]
                feat_ref[slot] = jnp.where(slot < count, one, jnp.zeros_like(one))

    def put(first, grad):
        last = first + grad.shape[0]
        for b in range(first // 144, (last - 1) // 144 + 1):
            lo, hi = max(first, 144 * b), min(last, 144 * (b + 1))
            piece = grad[lo - first:hi - first]
            keep_ref[b, lo - 144 * b:hi - 144 * b, :] = piece[:, :128]
            send_ref[b, lo - 144 * b:hi - 144 * b, :] = piece[:, 128:].astype(BF)

    temporal = lax.dot_general(pair_s[...], cotp_ref[...], (((0,), (0,)), ((), ())),
                               preferred_element_type=F32)
    for b in range(16):
        piece = temporal[b * 32:(b + 1) * 32]
        keep_ref[b, 144:, :] = piece[:, :128]
        send_ref[b, 144:, :] = piece[:, 128:].astype(BF)
    copies[STEPS].wait()
    for tap in range(TAPS):
        put(tap * C, jnp.dot(patcht_s[tap * C:(tap + 1) * C, :], gpre_s[...],
                             preferred_element_type=F32))


def make_patches(flags, plan, tiles, cotangent, pick, marks, perm):
    hbm = pl.BlockSpec(memory_space=pltpu.HBM)
    vmem = pl.BlockSpec(memory_space=pltpu.VMEM)
    smem = pl.BlockSpec(memory_space=pltpu.SMEM)
    return pl.pallas_call(
        patch_kernel,
        in_specs=[smem, smem, hbm, vmem, vmem, vmem, vmem],
        out_specs=[hbm, hbm, vmem, vmem],
        out_shape=[
            pltpu.HBM((ROWS, TAPS * C), BF),
            pltpu.HBM((TAPS * C, ROWS), BF),
            jax.ShapeDtypeStruct((COT_ROWS, C), BF),
            jax.ShapeDtypeStruct((COT_ROWS, C), BF),
        ],
        scratch_shapes=[
            pltpu.VMEM((OWNED, IN_PIX, C), BF),
            pltpu.VMEM((ROWS, TAPS * C), BF),
            pltpu.VMEM((TAPS * C, ROWS), BF),
            pltpu.SemaphoreType.DMA((STEPS,)),
            pltpu.SemaphoreType.DMA((2 * STEPS,)),
        ],
        compiler_params=pltpu.CompilerParams(vmem_limit_bytes=32 * 2**20),
        cost_estimate=pl.CostEstimate(flops=6 * 10**9, bytes_accessed=15 * 10**6, transcendentals=0),
        name="patches",
    )(flags, plan, pltpu.with_memory_space_constraint(tiles, pltpu.HBM), cotangent, pick, marks,
      perm)


def run_section(core, plan, got, other, cot_live, cot_perm, perm, patches, patches_t):
    hbm = pl.BlockSpec(memory_space=pltpu.HBM)
    vmem = pl.BlockSpec(memory_space=pltpu.VMEM)
    smem = pl.BlockSpec(memory_space=pltpu.SMEM)
    return pl.pallas_call(
        main_kernel,
        in_specs=[smem] * 2 + [vmem] * 5 + [hbm] * 2,
        out_specs=[vmem] * 3,
        out_shape=[
            jax.ShapeDtypeStruct((OWNED, OUT_PIX, C), BF),
            jax.ShapeDtypeStruct((16, 176, 128), F32),
            jax.ShapeDtypeStruct((16, 176, 128), BF),
        ],
        scratch_shapes=[
            pltpu.VMEM((ROWS, TAPS * C), BF),
            pltpu.VMEM((TAPS * C, ROWS), BF),
            pltpu.VMEM((TAPS * C, C), BF),
            pltpu.VMEM((2 * C, C), BF),
            pltpu.VMEM((COT_ROWS, 2 * C), BF),
            pltpu.VMEM((ROWS, C), BF),
            pltpu.SemaphoreType.DMA((STEPS + 1,)),
        ],
        compiler_params=pltpu.CompilerParams(vmem_limit_bytes=36 * 2**20),
        cost_estimate=pl.CostEstimate(flops=4 * 10**9, bytes_accessed=15 * 10**6, transcendentals=0),
        name="section",
    )(core, plan, got, other, cot_live, cot_perm, perm,
      pltpu.with_memory_space_constraint(patches, pltpu.HBM),
      pltpu.with_memory_space_constraint(patches_t, pltpu.HBM))


def spread_kernel(core_ref, spatial_hbm, temporal_hbm, out_hbm, rows_s, in_sems, out_sems):
    reads = [pltpu.make_async_copy(spatial_hbm, rows_s.at[pl.ds(0, 144)], in_sems.at[0]),
             pltpu.make_async_copy(temporal_hbm, rows_s.at[pl.ds(144, 32)], in_sems.at[1])]
    for copy in reads:
        copy.start()
    for copy in reads:
        copy.wait()

    def write(first):
        copies = [pltpu.make_async_copy(rows_s.at[pl.ds(first, SHARE)], out_hbm.at[b],
                                        out_sems.at[b])
                  for b in range(16)]
        for copy in copies:
            copy.start()
        for copy in copies:
            copy.wait()

    @pl.when(core_ref[0] == 0)
    def _():
        write(0)

    @pl.when(core_ref[0] != 0)
    def _():
        write(176 - SHARE)


def spread(core, spatial, temporal):
    smem = pl.BlockSpec(memory_space=pltpu.SMEM)
    hbm = pl.BlockSpec(memory_space=pltpu.HBM)
    return pl.pallas_call(
        spread_kernel,
        in_specs=[smem, hbm, hbm],
        out_specs=hbm,
        out_shape=pltpu.HBM((16, SHARE, C), BF),
        scratch_shapes=[
            pltpu.VMEM((176, C), BF),
            pltpu.SemaphoreType.DMA((2,)),
            pltpu.SemaphoreType.DMA((16,)),
        ],
        name="spread",
    )(core, pltpu.with_memory_space_constraint(spatial, pltpu.HBM),
      pltpu.with_memory_space_constraint(temporal, pltpu.HBM))


def permutation(core):
    row = lax.broadcasted_iota(jnp.int32, (C, C), 0)
    col = lax.broadcasted_iota(jnp.int32, (C, C), 1)
    wanted = ((col % 128) // 8) * 16 + jnp.bitwise_xor(core, col // 128) * 8 + col % 8
    return (row == wanted).astype(BF)


def per_device(tiles, cotangent, halo_flags, send_plan, spatial_weight, temporal_weight):
    core = lax.axis_index("dp") % 2
    siblings = [(i, i ^ 1) for i in range(32)]
    core_id = core.reshape(1).astype(jnp.int32)
    got = lax.all_to_all(spread(core_id, spatial_weight, temporal_weight), "bal", 0, 0)

    pick, marks = selection()
    perm = permutation(core)
    flags = halo_flags.T
    plan = send_plan[0].T
    patches, patches_t, cot_live, cot_perm = make_patches(
        flags, plan, tiles, cotangent, pick, marks, perm
    )
    got, cot_live = lax.optimization_barrier((got, cot_live))
    other = lax.ppermute(got, "dp", siblings)
    features, keep, send = run_section(
        core_id, plan, got, other, cot_live, cot_perm, perm,
        patches, patches_t
    )

    theirs = lax.ppermute(send, "dp", siblings)
    chip = (keep + theirs.astype(F32)).astype(BF)
    part = lax.all_to_all(chip, "bal", 0, 0)
    part = jnp.sum(part.astype(F32), axis=0)
    part = part.T.reshape(16, 8, 176)
    along_z = [[2 * z + c for z in range(16)] for c in range(2)]
    last = lax.all_to_all(part, "dp", 0, 0, axis_index_groups=along_z)
    total = jnp.sum(last, axis=0) * FACTOR
    return features, total[:, :144].T, total[:, 144:].T


def solution(mesh):
    in_specs = (
        P(("dp", "bal"), None, None),
        P(("dp", "bal"), None, None),
        P(("dp", "bal"), None),
        P(("dp", "bal"), None, None),
        P("bal", None),
        P("bal", None),
    )
    out_specs = (P(("dp", "bal"), None, None), P("bal", "dp"), P("bal", "dp"))
    return jax.shard_map(
        per_device, mesh=mesh, in_specs=in_specs, out_specs=out_specs, check_vma=False
    )
```

time: 92.4 us -> 87.2 us (0.944)
  local copies, waits for them, and re-layouts: 6.87 us -> 1.37 us
  Pallas kernels: 19.9 us -> 16.2 us
  waiting for transfers between devices: 8.42 us -> 11.3 us
  starting transfers between devices: 9.09 us -> 11 us
  other arithmetic: 1.74 us -> 0.8 us
    unnamed x10 -> x6, local copies, waits for them, and re-layouts: 4.3 us -> 0.01 us
    pallas_call x2 -> x3, Pallas kernels: 19.9 us -> 16.2 us  [the longest x1 7.39 us: run_section(): pl.pallas_call(main_kernel, in_specs=[smem] * 2 + [vmem] * 5 + [hbm] * 2,...]
    ppermute x1 -> x2, waiting for transfers between devices: 2.16 us -> 4.29 us  [the longest x1 2.25 us: per_device(): other = lax.ppermute(got, 'dp', siblings)]
    ppermute x1 -> x2, starting transfers between devices: 1.92 us -> 3.95 us  [the longest x1 2.04 us: per_device(): theirs = lax.ppermute(send, 'dp', siblings)]
    broadcast_in_dim x1 -> x0, local copies, waits for them, and re-layouts: 1.21 us -> none  [per_device(): blocks = jnp.broadcast_to(mine[None], (16,) + mine.shape)]
  transfers between devices with their start and end apart: 2 -> 3, of which waited for: 2 -> 3; matrix products, arithmetic and copies ran while one was open for 1% -> 1% of each run, Pallas kernels for 13% -> 8%
where the time goes in v2:
time: 87.2 us; the launch traced here: 86.8 us
  blocking collectives  45.3 us (52%)
  Pallas kernels  16.2 us (19%)
  waiting for transfers between devices  11.3 us (13%)
  starting transfers between devices  11 us (13%)
  local copies, waits for them, and re-layouts  1.37 us (2%)
    all_to_all x1, blocking collectives, per_device(): last = lax.all_to_all(part, 'dp', 0, 0, axis_index_groups=along_z)  28.5 us
    all_to_all x1, blocking collectives, per_device(): part = lax.all_to_all(chip, 'bal', 0, 0)  16.8 us
    pallas_call x1, Pallas kernels, run_section(): pl.pallas_call(main_kernel, in_specs=[smem] * 2 + [vmem] * 5 + [hbm] * 2,...  7.39 us
    all_to_all x1, starting transfers between devices, per_device(): lax.all_to_all(spread(core_id, spatial_weight, temporal_weight), 'bal', 0...  7.05 us
    all_to_all x1, waiting for transfers between devices, per_device(): lax.all_to_all(spread(core_id, spatial_weight, temporal_weight), 'bal', 0...  6.96 us
    pallas_call x1, Pallas kernels, make_patches(): pl.pallas_call(patch_kernel, in_specs=[smem, smem, hbm, vmem, vmem, vmem,...  6.87 us
    ppermute x1, waiting for transfers between devices, per_device(): other = lax.ppermute(got, 'dp', siblings)  2.25 us
    ppermute x1, starting transfers between devices, per_device(): theirs = lax.ppermute(send, 'dp', siblings)  2.04 us
  transfers between devices with their start and end apart: 3, of which 3 were waited for; matrix products, arithmetic and copies ran while one was open for 1% of the time, Pallas kernels for 8%

profile of v2, /device:TPU:32, one launch (start us, length us, event | category | flops | bytes accessed | tf_op | source)
XLA Modules:
  0.0 86.8 jit_solution(13086615567476233400)
XLA Ops:
  0.6 0.0 copy-start.2
  0.6 0.0 copy-start.1
  0.7 0.0 copy-start
  0.7 2.0 %spread.1 = bf16[16,96,256]{2,1,0:T(8,128)(2,1)} custom-call(s32[1]{0:T(128)} %bitcast.core_ref, bf16[144,256]{1,0:T(8,128)(2,1)} %spatial_hbm.1, bf16[32,256]{1,0:T(8,128)(2,1)} %temporal_hbm.1), custom_call_target="tpu_custom_call" | custom-call | tf_op jit(solution)/shard_map/spread/pallas_call | solution.py:272
  2.7 7.0 %all-to-all-start = ((bf16[16,96,256]{2,1,0:T(8,128)(2,1)}), bf16[16,96,256]{2,1,0:T(8,128)(2,1)S(1)}, u32[]{:S(2)}, u32[]{:S(2)}) async-start(bf16[16,96,256]{2,1,0:T(8,128)(2,1)} %spread.1), calls=%async_computation | async-start | bytes 1572864 | tf_op jit(solution)/shard_map/all_to_all | solution.py:298
  9.8 0.3 fusion.35.pick_ref
  10.2 0.1 fusion.49.mark_ref
  10.3 0.0 copy-done.2
  10.3 0.0 copy-done.1
  10.4 0.0 copy-done
  10.4 6.9 %patches.1 = (bf16[1152,2304]{1,0:T(8,128)(2,1)}, bf16[2304,1152]{1,0:T(8,128)(2,1)}, bf16[768,256]{1,0:T(8,128)(2,1)S(1)}, bf16[768,256]{1,0:T(8,128)(2,1)S(1)}) custom-call(s32[3,23]{1,0:T(4,128)S(1)} %bitcast.11, s32[2,16]{1,0:T(2,128)S(1)} %bitcast.12, bf16[23,270,256]{2,1,0:T(8,128)(2,1)} %tiles_hbm.1, bf16[23,32,256]{2,1,0:T(8,128)(2,1)S(1)} %copy-done, ...), custom_call_target="tpu_custom_call" | custom-call | flops 6000000000 | bytes 15000000 | tf_op jit(solution)/shard_map/patches/pallas_call | solution.py:189
  17.3 7.0 %all-to-all-done.got_ref = bf16[16,96,256]{2,1,0:T(8,128)(2,1)S(1)} async-done(((bf16[16,96,256]{2,1,0:T(8,128)(2,1)}), bf16[16,96,256]{2,1,0:T(8,128)(2,1)S(1)}, u32[]{:S(2)}, u32[]{:S(2)}) %all-to-all-start) | async-done | bytes 786464 | tf_op jit(solution)/shard_map/all_to_all | solution.py:298
  24.2 1.9 %collective-permute-start = (bf16[16,96,256]{2,1,0:T(8,128)(2,1)S(1)}, bf16[16,96,256]{2,1,0:T(8,128)(2,1)S(1)}, u32[]{:S(2)}, u32[]{:S(2)}) collective-permute-start(bf16[16,96,256]{2,1,0:T(8,128)(2,1)S(1)} %all-to-all-done.got_ref), channel_id=1, source_target_pairs={{0,16},{16,0},{32,48},{48,32},{64,80},{80,64},{96,112},{112,96},{1... | collective-permute-start | bytes 2359304 | tf_op jit(solution)/shard_map/ppermute | solution.py:308
  26.1 2.3 %collective-permute-done.other_ref = bf16[16,96,256]{2,1,0:T(8,128)(2,1)S(1)} collective-permute-done((bf16[16,96,256]{2,1,0:T(8,128)(2,1)S(1)}, bf16[16,96,256]{2,1,0:T(8,128)(2,1)S(1)}, u32[]{:S(2)}, u32[]{:S(2)}) %collective-permute-start) | collective-permute-done | bytes 786464 | tf_op jit(solution)/shard_map/ppermute | solution.py:308
  28.4 7.4 %section.1 = (bf16[23,32,256]{2,1,0:T(8,128)(2,1)}, f32[16,176,128]{2,1,0:T(8,128)S(1)}, bf16[16,176,128]{2,1,0:T(8,128)(2,1)S(1)}) custom-call(s32[1]{0:T(128)} %bitcast.core_ref, s32[2,16]{1,0:T(2,128)S(1)} %bitcast.13, bf16[16,96,256]{2,1,0:T(8,128)(2,1)S(1)} %all-to-all-done.got_ref, bf16[16,96,256]{2,1,0:T(8,128)(2,1)S(1)} %collective-permute-done.other_ref, ...), custom_call_target="tpu_custom_call" | custom-call | flops 4000000000 | bytes 15000000 | tf_op jit(solution)/shard_map/section/pallas_call | solution.py:217
  35.8 2.0 %collective-permute-start.1 = (bf16[16,176,128]{2,1,0:T(8,128)(2,1)S(1)}, bf16[16,176,128]{2,1,0:T(8,128)(2,1)S(1)}, u32[]{:S(2)}, u32[]{:S(2)}) collective-permute-start(bf16[16,176,128]{2,1,0:T(8,128)(2,1)S(1)} %get-tuple-element.20), channel_id=1, source_target_pairs={{0,16},{16,0},{32,48},{48,32},{64,80},{80,64},{96,112},{112,96},{1... | collective-permute-start | bytes 2162696 | tf_op jit(solution)/shard_map/ppermute | solution.py:314
  37.8 2.0 %collective-permute-done.1 = bf16[16,176,128]{2,1,0:T(8,128)(2,1)S(1)} collective-permute-done((bf16[16,176,128]{2,1,0:T(8,128)(2,1)S(1)}, bf16[16,176,128]{2,1,0:T(8,128)(2,1)S(1)}, u32[]{:S(2)}, u32[]{:S(2)}) %collective-permute-start.1) | collective-permute-done | bytes 720928 | tf_op jit(solution)/shard_map/ppermute | solution.py:314
  39.9 0.1 add_convert_fusion
  40.0 16.8 %all_to_all.15 = bf16[16,176,128]{2,1,0:T(8,128)(2,1)S(1)} all-to-all(bf16[16,176,128]{2,1,0:T(8,128)(2,1)S(1)} %add_convert_fusion), channel_id=1, replica_groups=mesh['dp'=32,'bal'=16] {'bal'}, dimensions={0} | all-to-all | bytes 1441792 | tf_op jit(solution)/shard_map/all_to_all | solution.py:316
  56.8 0.1 convert_reduce_fusion
  56.9 0.1 copy.9
  57.0 28.5 %all_to_all.16 = f32[16,8,176]{2,1,0:T(8,128)S(1)} all-to-all(f32[16,8,176]{2,1,0:T(8,128)S(1)} %bitcast.14), channel_id=1, replica_groups={{0,32,64,96,128,160,192,224,256,288,320,352,384,416,448,480},{16,48,80,..., dimensions={0} | all-to-all | bytes 180224 | tf_op jit(solution)/shard_map/all_to_all | solution.py:320
  85.6 0.7 slice_bitcast_fusion.1
  86.2 0.6 slice_bitcast_fusion
  (14 shorter events, 0.1 us)
Async XLA Ops:
  0.6 9.7 %copy-start.2 = (s32[1,16,2]{1,2,0:T(2,128)S(1)}, s32[1,16,2]{1,2,0:T(2,128)}, u32[]{:S(2)}) copy-start(s32[1,16,2]{1,2,0:T(2,128)} %param.9) | copy-start | bytes 388
  0.6 9.7 %copy-start.1 = (s32[23,3]{0,1:T(4,128)S(1)}, s32[23,3]{0,1:T(4,128)}, u32[]{:S(2)}) copy-start(s32[23,3]{0,1:T(4,128)} %param.8) | copy-start | bytes 832
  0.7 9.7 %copy-start = (bf16[23,32,256]{2,1,0:T(8,128)(2,1)S(1)}, bf16[23,32,256]{2,1,0:T(8,128)(2,1)}, u32[]{:S(2)}) copy-start(bf16[23,32,256]{2,1,0:T(8,128)(2,1)} %cot_ref.1) | copy-start | bytes 1130500
  2.7 21.6 %all-to-all-start = ((bf16[16,96,256]{2,1,0:T(8,128)(2,1)}), bf16[16,96,256]{2,1,0:T(8,128)(2,1)S(1)}, u32[]{:S(2)}, u32[]{:S(2)}) async-start(bf16[16,96,256]{2,1,0:T(8,128)(2,1)} %spread.1), calls=%async_computation | async-start | bytes 1572864 | tf_op jit(solution)/shard_map/all_to_all | solution.py:298
  24.2 4.2 %collective-permute-start = (bf16[16,96,256]{2,1,0:T(8,128)(2,1)S(1)}, bf16[16,96,256]{2,1,0:T(8,128)(2,1)S(1)}, u32[]{:S(2)}, u32[]{:S(2)}) collective-permute-start(bf16[16,96,256]{2,1,0:T(8,128)(2,1)S(1)} %all-to-all-done.got_ref), channel_id=1, source_target_pairs={{0,16},{16,0},{32,48},{48,32},{64,80},{80,64},{96,112},{112,96},{1... | collective-permute-start | bytes 2359304 | tf_op jit(solution)/shard_map/ppermute | solution.py:308
  35.8 4.1 %collective-permute-start.1 = (bf16[16,176,128]{2,1,0:T(8,128)(2,1)S(1)}, bf16[16,176,128]{2,1,0:T(8,128)(2,1)S(1)}, u32[]{:S(2)}, u32[]{:S(2)}) collective-permute-start(bf16[16,176,128]{2,1,0:T(8,128)(2,1)S(1)} %get-tuple-element.20), channel_id=1, source_target_pairs={{0,16},{16,0},{32,48},{48,32},{64,80},{80,64},{96,112},{112,96},{1... | collective-permute-start | bytes 2162696 | tf_op jit(solution)/shard_map/ppermute | solution.py:314

commit v3 on v2

--- a/solution.py
+++ b/solution.py
@@ -22,6 +22,7 @@
 ROWS = PAD_TILES * ACT_PIX
 GROUP_ROWS = GROUP * ACT_PIX
 DOT_ROWS = 192
+EARLY_ROWS = 2 * GROUP_ROWS
 COT_ROWS = PAD_TILES * OUT_PIX
 GROUP_COT = GROUP * OUT_PIX
 WINDOWS = ((0, 128), (80, 128), (160, 110))
@@ -104,13 +105,38 @@
         write.wait()
 
 
-def main_kernel(core_ref, plan_ref, got_ref, other_ref, cotl_ref, cotp_ref, perm_ref,
+def fetch_kernel(patch_hbm, early_ref, sems):
+    spans = [pl.ds(r, 96) for r in range(0, EARLY_ROWS, 96)]
+    copies = [pltpu.make_async_copy(patch_hbm.at[span, :], early_ref.at[span, :], sems.at[k])
+              for k, span in enumerate(spans)]
+    for copy in copies:
+        copy.start()
+    for copy in copies:
+        copy.wait()
+
+
+def fetch(patches):
+    return pl.pallas_call(
+        fetch_kernel,
+        in_specs=[pl.BlockSpec(memory_space=pltpu.HBM)],
+        out_specs=pl.BlockSpec(memory_space=pltpu.VMEM),
+        out_shape=jax.ShapeDtypeStruct((EARLY_ROWS, TAPS * C), BF),
+        scratch_shapes=[pltpu.SemaphoreType.DMA((EARLY_ROWS // 96,))],
+        compiler_params=pltpu.CompilerParams(vmem_limit_bytes=8 * 2**20),
+        cost_estimate=pl.CostEstimate(flops=0, bytes_accessed=8 * 10**6, transcendentals=0),
+        name="fetch",
+    )(pltpu.with_memory_space_constraint(patches, pltpu.HBM))
+
+
+def main_kernel(core_ref, plan_ref, got_ref, other_ref, cotl_ref, cotp_ref, perm_ref, early_ref,
                 patch_hbm, patcht_hbm, feat_ref, keep_ref, send_ref,
-                patch_s, patcht_s, spatial_s, temporal_s, pair_s, gpre_s, sems):
-    spans = [pl.ds(g * GROUP_ROWS, GROUP_ROWS) for g in range(STEPS)]
-    copies = [pltpu.make_async_copy(patch_hbm.at[span, :], patch_s.at[span, :], sems.at[g])
-              for g, span in enumerate(spans)]
-    copies.append(pltpu.make_async_copy(patcht_hbm, patcht_s, sems.at[STEPS]))
+                late_s, patcht_s, spatial_s, temporal_s, pair_s, gpre_s, sems):
+    copies = [pltpu.make_async_copy(patch_hbm.at[pl.ds(EARLY_ROWS + r, 96), :],
+                                    late_s.at[pl.ds(r, 96), :], sems.at[r // 96])
+              for r in range(0, GROUP_ROWS, 96)]
+    copies += [pltpu.make_async_copy(patcht_hbm.at[pl.ds(tap * C, C), :],
+                                     patcht_s.at[pl.ds(tap * C, C), :], sems.at[4 + tap])
+               for tap in range(TAPS)]
     for copy in copies:
         copy.start()
     count = live_count(plan_ref)
@@ -130,12 +156,16 @@
         place(other_ref, got_ref)
 
     for g in range(STEPS):
-        copies[g].wait()
+        if g == STEPS - 1:
+            for copy in copies:
+                copy.wait()
+        patch_ref = late_s if g == STEPS - 1 else early_ref
+        base = 0 if g == STEPS - 1 else g * GROUP_ROWS
         rows = slice(g * GROUP_ROWS, (g + 1) * GROUP_ROWS)
         cells = slice(g * GROUP_COT, (g + 1) * GROUP_COT)
         pre = jnp.concatenate([
-            jnp.dot(patch_s[r:r + DOT_ROWS, :], spatial_s[...], preferred_element_type=F32)
-            for r in range(g * GROUP_ROWS, (g + 1) * GROUP_ROWS, DOT_ROWS)
+            jnp.dot(patch_ref[r:r + DOT_ROWS, :], spatial_s[...], preferred_element_type=F32)
+            for r in range(base, base + GROUP_ROWS, DOT_ROWS)
         ], axis=0)
         sig = 1.0 / (1.0 + jnp.exp(-pre))
         act = (pre * sig).astype(BF)
@@ -176,7 +206,6 @@
         piece = temporal[b * 32:(b + 1) * 32]
         keep_ref[b, 144:, :] = piece[:, :128]
         send_ref[b, 144:, :] = piece[:, 128:].astype(BF)
-    copies[STEPS].wait()
     for tap in range(TAPS):
         put(tap * C, jnp.dot(patcht_s[tap * C:(tap + 1) * C, :], gpre_s[...],
                              preferred_element_type=F32))
@@ -210,13 +239,13 @@
       perm)
 
 
-def run_section(core, plan, got, other, cot_live, cot_perm, perm, patches, patches_t):
+def run_section(core, plan, got, other, cot_live, cot_perm, perm, early, patches, patches_t):
     hbm = pl.BlockSpec(memory_space=pltpu.HBM)
     vmem = pl.BlockSpec(memory_space=pltpu.VMEM)
     smem = pl.BlockSpec(memory_space=pltpu.SMEM)
     return pl.pallas_call(
         main_kernel,
-        in_specs=[smem] * 2 + [vmem] * 5 + [hbm] * 2,
+        in_specs=[smem] * 2 + [vmem] * 6 + [hbm] * 2,
         out_specs=[vmem] * 3,
         out_shape=[
             jax.ShapeDtypeStruct((OWNED, OUT_PIX, C), BF),
@@ -224,38 +253,34 @@
             jax.ShapeDtypeStruct((16, 176, 128), BF),
         ],
         scratch_shapes=[
-            pltpu.VMEM((ROWS, TAPS * C), BF),
+            pltpu.VMEM((GROUP_ROWS, TAPS * C), BF),
             pltpu.VMEM((TAPS * C, ROWS), BF),
             pltpu.VMEM((TAPS * C, C), BF),
             pltpu.VMEM((2 * C, C), BF),
             pltpu.VMEM((COT_ROWS, 2 * C), BF),
             pltpu.VMEM((ROWS, C), BF),
-            pltpu.SemaphoreType.DMA((STEPS + 1,)),
+            pltpu.SemaphoreType.DMA((4 + TAPS,)),
         ],
         compiler_params=pltpu.CompilerParams(vmem_limit_bytes=36 * 2**20),
         cost_estimate=pl.CostEstimate(flops=4 * 10**9, bytes_accessed=15 * 10**6, transcendentals=0),
         name="section",
-    )(core, plan, got, other, cot_live, cot_perm, perm,
+    )(core, plan, got, other, cot_live, cot_perm, perm, early,
       pltpu.with_memory_space_constraint(patches, pltpu.HBM),
       pltpu.with_memory_space_constraint(patches_t, pltpu.HBM))
 
 
-def spread_kernel(core_ref, spatial_hbm, temporal_hbm, out_hbm, rows_s, in_sems, out_sems):
-    reads = [pltpu.make_async_copy(spatial_hbm, rows_s.at[pl.ds(0, 144)], in_sems.at[0]),
-             pltpu.make_async_copy(temporal_hbm, rows_s.at[pl.ds(144, 32)], in_sems.at[1])]
+def spread_kernel(core_ref, spatial_hbm, temporal_hbm, out_ref, rows_s, sems):
+    reads = [pltpu.make_async_copy(spatial_hbm, rows_s.at[pl.ds(0, 144)], sems.at[0]),
+             pltpu.make_async_copy(temporal_hbm, rows_s.at[pl.ds(144, 32)], sems.at[1])]
     for copy in reads:
         copy.start()
     for copy in reads:
         copy.wait()
 
     def write(first):
-        copies = [pltpu.make_async_copy(rows_s.at[pl.ds(first, SHARE)], out_hbm.at[b],
-                                        out_sems.at[b])
-                  for b in range(16)]
-        for copy in copies:
-            copy.start()
-        for copy in copies:
-            copy.wait()
+        mine = rows_s[first:first + SHARE, :]
+        for b in range(16):
+            out_ref[b] = mine
 
     @pl.when(core_ref[0] == 0)
     def _():
@@ -272,16 +297,48 @@
     return pl.pallas_call(
         spread_kernel,
         in_specs=[smem, hbm, hbm],
-        out_specs=hbm,
-        out_shape=pltpu.HBM((16, SHARE, C), BF),
+        out_specs=pl.BlockSpec(memory_space=pltpu.VMEM),
+        out_shape=jax.ShapeDtypeStruct((16, SHARE, C), BF),
         scratch_shapes=[
             pltpu.VMEM((176, C), BF),
             pltpu.SemaphoreType.DMA((2,)),
-            pltpu.SemaphoreType.DMA((16,)),
-        ],
+        ],
+        compiler_params=pltpu.CompilerParams(vmem_limit_bytes=8 * 2**20),
         name="spread",
     )(core, pltpu.with_memory_space_constraint(spatial, pltpu.HBM),
       pltpu.with_memory_space_constraint(temporal, pltpu.HBM))
+
+
+def finish_kernel(part_ref, spatial_hbm, temporal_hbm, spatial_s, temporal_s, sems):
+    total = part_ref[0]
+    for z in range(1, part_ref.shape[0]):
+        total = total + part_ref[z]
+    total = total * FACTOR
+    spatial_s[...] = total[:, :144]
+    temporal_s[...] = total[:, 144:]
+    copies = [pltpu.make_async_copy(spatial_s, spatial_hbm, sems.at[0]),
+              pltpu.make_async_copy(temporal_s, temporal_hbm, sems.at[1])]
+    for copy in copies:
+        copy.start()
+    for copy in copies:
+        copy.wait()
+
+
+def finish(part):
+    hbm = pl.BlockSpec(memory_space=pltpu.HBM)
+    return pl.pallas_call(
+        finish_kernel,
+        in_specs=[pl.BlockSpec(memory_space=pltpu.VMEM)],
+        out_specs=[hbm, hbm],
+        out_shape=[pltpu.HBM((8, 144), F32), pltpu.HBM((8, 32), F32)],
+        scratch_shapes=[
+            pltpu.VMEM((8, 144), F32),
+            pltpu.VMEM((8, 32), F32),
+            pltpu.SemaphoreType.DMA((2,)),
+        ],
+        compiler_params=pltpu.CompilerParams(vmem_limit_bytes=4 * 2**20),
+        name="finish",
+    )(part)
 
 
 def permutation(core):
@@ -304,11 +361,10 @@
     patches, patches_t, cot_live, cot_perm = make_patches(
         flags, plan, tiles, cotangent, pick, marks, perm
     )
-    got, cot_live = lax.optimization_barrier((got, cot_live))
+    got, patches, patches_t = lax.optimization_barrier((got, patches, patches_t))
     other = lax.ppermute(got, "dp", siblings)
     features, keep, send = run_section(
-        core_id, plan, got, other, cot_live, cot_perm, perm,
-        patches, patches_t
+        core_id, plan, got, other, cot_live, cot_perm, perm, fetch(patches), patches, patches_t
     )
 
     theirs = lax.ppermute(send, "dp", siblings)
@@ -318,8 +374,8 @@
     part = part.T.reshape(16, 8, 176)
     along_z = [[2 * z + c for z in range(16)] for c in range(2)]
     last = lax.all_to_all(part, "dp", 0, 0, axis_index_groups=along_z)
-    total = jnp.sum(last, axis=0) * FACTOR
-    return features, total[:, :144].T, total[:, 144:].T
+    spatial_t, temporal_t = finish(last)
+    return features, spatial_t.T, temporal_t.T
 
 
 def solution(mesh):

time: 87.2 us -> 85.7 us (0.983)
  waiting for transfers between devices: 11.3 us -> 9.09 us
  Pallas kernels: 16.2 us -> 17.9 us
  local copies, waits for them, and re-layouts: 1.37 us -> 0.11 us
    ppermute x1, waiting for transfers between devices: 2.25 us -> 0.23 us  [per_device(): other = lax.ppermute(got, 'dp', siblings)]
    pallas_call x2 -> x4, Pallas kernels: 9.37 us -> 11 us  [the longest x1 6.4 us: run_section(): pl.pallas_call(main_kernel, in_specs=[smem] * 2 + [vmem] * 6 + [hbm] * 2,...]
    transpose x2 -> x0, local copies, waits for them, and re-layouts: 1.26 us -> none  [per_device(): return (features, total[:, :144].T, total[:, 144:].T)]
  transfers between devices with their start and end apart: 3 -> 3, of which waited for: 3 -> 3; matrix products, arithmetic and copies ran while one was open for 1% -> 1% of each run, Pallas kernels for 8% -> 10%
where the time goes in v3:
time: 85.7 us; the launch traced here: 85.4 us
  blocking collectives  45.5 us (53%)
  Pallas kernels  17.9 us (21%)
  starting transfers between devices  11.2 us (13%)
  waiting for transfers between devices  9.09 us (11%)
    all_to_all x1, blocking collectives, per_device(): last = lax.all_to_all(part, 'dp', 0, 0, axis_index_groups=along_z)  28.5 us
    all_to_all x1, blocking collectives, per_device(): part = lax.all_to_all(chip, 'bal', 0, 0)  17 us
    all_to_all x1, starting transfers between devices, per_device(): lax.all_to_all(spread(core_id, spatial_weight, temporal_weight), 'bal', 0...  7.05 us
    all_to_all x1, waiting for transfers between devices, per_device(): lax.all_to_all(spread(core_id, spatial_weight, temporal_weight), 'bal', 0...  6.99 us
    pallas_call x1, Pallas kernels, make_patches(): pl.pallas_call(patch_kernel, in_specs=[smem, smem, hbm, vmem, vmem, vmem,...  6.85 us
    pallas_call x1, Pallas kernels, run_section(): pl.pallas_call(main_kernel, in_specs=[smem] * 2 + [vmem] * 6 + [hbm] * 2,...  6.4 us
    ppermute x1, starting transfers between devices, per_device(): theirs = lax.ppermute(send, 'dp', siblings)  2.2 us
    pallas_call x1, Pallas kernels, fetch(): pl.pallas_call(fetch_kernel, in_specs=[pl.BlockSpec(memory_space=pltpu.HB...  2.02 us
  transfers between devices with their start and end apart: 3, of which 3 were waited for; matrix products, arithmetic and copies ran while one was open for 1% of the time, Pallas kernels for 10%

profile of v3, /device:TPU:32, one launch (start us, length us, event | category | flops | bytes accessed | tf_op | source)
XLA Modules:
  0.0 85.4 jit_solution(15257478461275541265)
XLA Ops:
  0.6 0.0 copy-start
  0.6 0.0 copy-start.2
  0.7 0.0 copy-start.1
  0.7 1.9 %spread.1 = bf16[16,96,256]{2,1,0:T(8,128)(2,1)} custom-call(s32[1]{0:T(128)} %bitcast.core_ref, bf16[144,256]{1,0:T(8,128)(2,1)} %spatial_hbm.1, bf16[32,256]{1,0:T(8,128)(2,1)} %temporal_hbm.1), custom_call_target="tpu_custom_call" | custom-call | tf_op jit(solution)/shard_map/spread/pallas_call | solution.py:297
  2.6 7.0 %all-to-all-start = ((bf16[16,96,256]{2,1,0:T(8,128)(2,1)}), bf16[16,96,256]{2,1,0:T(8,128)(2,1)S(1)}, u32[]{:S(2)}, u32[]{:S(2)}) async-start(bf16[16,96,256]{2,1,0:T(8,128)(2,1)} %spread.1), calls=%async_computation | async-start | bytes 1572864 | tf_op jit(solution)/shard_map/all_to_all | solution.py:355
  9.8 0.3 fusion.35.pick_ref
  10.2 0.1 fusion.49.mark_ref
  10.3 0.0 copy-done
  10.3 0.0 copy-done.2
  10.3 0.0 copy-done.1
  10.3 6.8 %patches.1 = (bf16[1152,2304]{1,0:T(8,128)(2,1)}, bf16[2304,1152]{1,0:T(8,128)(2,1)}, bf16[768,256]{1,0:T(8,128)(2,1)S(1)}, bf16[768,256]{1,0:T(8,128)(2,1)S(1)}) custom-call(s32[3,23]{1,0:T(4,128)S(1)} %bitcast.11, s32[2,16]{1,0:T(2,128)S(1)} %bitcast.9, bf16[23,270,256]{2,1,0:T(8,128)(2,1)} %tiles_hbm.1, bf16[23,32,256]{2,1,0:T(8,128)(2,1)S(1)} %copy-done.1, ...), custom_call_target="tpu_custom_call" | custom-call | flops 6000000000 | bytes 15000000 | tf_op jit(solution)/shard_map/patches/pallas_call | solution.py:218
  17.2 7.0 %all-to-all-done.got_ref = bf16[16,96,256]{2,1,0:T(8,128)(2,1)S(1)} async-done(((bf16[16,96,256]{2,1,0:T(8,128)(2,1)}), bf16[16,96,256]{2,1,0:T(8,128)(2,1)S(1)}, u32[]{:S(2)}, u32[]{:S(2)}) %all-to-all-start) | async-done | bytes 786464 | tf_op jit(solution)/shard_map/all_to_all | solution.py:355
  24.2 1.9 %collective-permute-start = (bf16[16,96,256]{2,1,0:T(8,128)(2,1)S(1)}, bf16[16,96,256]{2,1,0:T(8,128)(2,1)S(1)}, u32[]{:S(2)}, u32[]{:S(2)}) collective-permute-start(bf16[16,96,256]{2,1,0:T(8,128)(2,1)S(1)} %all-to-all-done.got_ref), channel_id=1, source_target_pairs={{0,16},{16,0},{32,48},{48,32},{64,80},{80,64},{96,112},{112,96},{1... | collective-permute-start | bytes 2359304 | tf_op jit(solution)/shard_map/ppermute | solution.py:365
  26.1 2.0 %fetch.1.early_ref = bf16[768,2304]{1,0:T(8,128)(2,1)S(1)} custom-call(bf16[1152,2304]{1,0:T(8,128)(2,1)} %get-tuple-element.20.patch_hbm), custom_call_target="tpu_custom_call" | custom-call | bytes 8000000 | tf_op jit(solution)/shard_map/fetch/pallas_call | solution.py:119
  28.1 0.2 collective-permute-done.other_ref
  28.3 6.4 %section.1 = (bf16[23,32,256]{2,1,0:T(8,128)(2,1)}, f32[16,176,128]{2,1,0:T(8,128)S(1)}, bf16[16,176,128]{2,1,0:T(8,128)(2,1)S(1)}) custom-call(s32[1]{0:T(128)} %bitcast.core_ref, s32[2,16]{1,0:T(2,128)S(1)} %bitcast.10, bf16[16,96,256]{2,1,0:T(8,128)(2,1)S(1)} %all-to-all-done.got_ref, bf16[16,96,256]{2,1,0:T(8,128)(2,1)S(1)} %collective-permute-done.other_ref, ...), custom_call_target="tpu_custom_call" | custom-call | flops 4000000000 | bytes 15000000 | tf_op jit(solution)/shard_map/section/pallas_call | solution.py:246
  34.7 2.2 %collective-permute-start.1 = (bf16[16,176,128]{2,1,0:T(8,128)(2,1)S(1)}, bf16[16,176,128]{2,1,0:T(8,128)(2,1)S(1)}, u32[]{:S(2)}, u32[]{:S(2)}) collective-permute-start(bf16[16,176,128]{2,1,0:T(8,128)(2,1)S(1)} %get-tuple-element.24), channel_id=1, source_target_pairs={{0,16},{16,0},{32,48},{48,32},{64,80},{80,64},{96,112},{112,96},{1... | collective-permute-start | bytes 2162696 | tf_op jit(solution)/shard_map/ppermute | solution.py:370
  36.9 1.9 %collective-permute-done.1 = bf16[16,176,128]{2,1,0:T(8,128)(2,1)S(1)} collective-permute-done((bf16[16,176,128]{2,1,0:T(8,128)(2,1)S(1)}, bf16[16,176,128]{2,1,0:T(8,128)(2,1)S(1)}, u32[]{:S(2)}, u32[]{:S(2)}) %collective-permute-start.1) | collective-permute-done | bytes 720928 | tf_op jit(solution)/shard_map/ppermute | solution.py:370
  38.8 0.2 add_convert_fusion
  39.0 17.0 %all_to_all.15 = bf16[16,176,128]{2,1,0:T(8,128)(2,1)S(1)} all-to-all(bf16[16,176,128]{2,1,0:T(8,128)(2,1)S(1)} %add_convert_fusion), channel_id=1, replica_groups=mesh['dp'=32,'bal'=16] {'bal'}, dimensions={0} | all-to-all | bytes 1441792 | tf_op jit(solution)/shard_map/all_to_all | solution.py:372
  56.0 0.1 convert_reduce_fusion
  56.1 0.1 copy.9
  56.2 28.5 %all_to_all.16.part_ref = f32[16,8,176]{2,1,0:T(8,128)S(1)} all-to-all(f32[16,8,176]{2,1,0:T(8,128)S(1)} %bitcast.12), channel_id=1, replica_groups={{0,32,64,96,128,160,192,224,256,288,320,352,384,416,448,480},{16,48,80,..., dimensions={0} | all-to-all | bytes 180224 | tf_op jit(solution)/shard_map/all_to_all | solution.py:376
  84.7 0.7 finish.1
  (12 shorter events, 0.1 us)
Async XLA Ops:
  0.6 9.7 %copy-start = (s32[1,16,2]{1,2,0:T(2,128)S(1)}, s32[1,16,2]{1,2,0:T(2,128)}, u32[]{:S(2)}) copy-start(s32[1,16,2]{1,2,0:T(2,128)} %param.9) | copy-start | bytes 388
  0.6 9.7 %copy-start.2 = (s32[23,3]{0,1:T(4,128)S(1)}, s32[23,3]{0,1:T(4,128)}, u32[]{:S(2)}) copy-start(s32[23,3]{0,1:T(4,128)} %param.8) | copy-start | bytes 832
  0.7 9.7 %copy-start.1 = (bf16[23,32,256]{2,1,0:T(8,128)(2,1)S(1)}, bf16[23,32,256]{2,1,0:T(8,128)(2,1)}, u32[]{:S(2)}) copy-start(bf16[23,32,256]{2,1,0:T(8,128)(2,1)} %cot_ref.1) | copy-start | bytes 1130500
  2.6 21.6 %all-to-all-start = ((bf16[16,96,256]{2,1,0:T(8,128)(2,1)}), bf16[16,96,256]{2,1,0:T(8,128)(2,1)S(1)}, u32[]{:S(2)}, u32[]{:S(2)}) async-start(bf16[16,96,256]{2,1,0:T(8,128)(2,1)} %spread.1), calls=%async_computation | async-start | bytes 1572864 | tf_op jit(solution)/shard_map/all_to_all | solution.py:355
  24.2 4.2 %collective-permute-start = (bf16[16,96,256]{2,1,0:T(8,128)(2,1)S(1)}, bf16[16,96,256]{2,1,0:T(8,128)(2,1)S(1)}, u32[]{:S(2)}, u32[]{:S(2)}) collective-permute-start(bf16[16,96,256]{2,1,0:T(8,128)(2,1)S(1)} %all-to-all-done.got_ref), channel_id=1, source_target_pairs={{0,16},{16,0},{32,48},{48,32},{64,80},{80,64},{96,112},{112,96},{1... | collective-permute-start | bytes 2359304 | tf_op jit(solution)/shard_map/ppermute | solution.py:365
  34.7 4.1 %collective-permute-start.1 = (bf16[16,176,128]{2,1,0:T(8,128)(2,1)S(1)}, bf16[16,176,128]{2,1,0:T(8,128)(2,1)S(1)}, u32[]{:S(2)}, u32[]{:S(2)}) collective-permute-start(bf16[16,176,128]{2,1,0:T(8,128)(2,1)S(1)} %get-tuple-element.24), channel_id=1, source_target_pairs={{0,16},{16,0},{32,48},{48,32},{64,80},{80,64},{96,112},{112,96},{1... | collective-permute-start | bytes 2162696 | tf_op jit(solution)/shard_map/ppermute | solution.py:370

commit v4 on v3

--- a/solution.py
+++ b/solution.py
@@ -22,7 +22,7 @@
 ROWS = PAD_TILES * ACT_PIX
 GROUP_ROWS = GROUP * ACT_PIX
 DOT_ROWS = 192
-EARLY_ROWS = 2 * GROUP_ROWS
+REST_ROWS = ROWS - GROUP_ROWS
 COT_ROWS = PAD_TILES * OUT_PIX
 GROUP_COT = GROUP * OUT_PIX
 WINDOWS = ((0, 128), (80, 128), (160, 110))
@@ -58,9 +58,9 @@
     return count + 1
 
 
-def patch_kernel(flags_ref, plan_ref, tiles_hbm, cot_ref, pick_ref, mark_ref, perm_ref,
-                 patch_hbm, patcht_hbm, cotl_ref, cotp_ref,
-                 tiles_s, patch_ref, patcht_ref, sems, out_sems):
+def patch_kernel(flags_ref, plan_ref, tiles_hbm, cot_ref, pick_ref, mark_ref,
+                 first_ref, patch_hbm, patcht_hbm, cotl_ref,
+                 tiles_s, patch_s, patcht_ref, sems, out_sems):
     copies = []
     for g in range(STEPS):
         first, last = g * GROUP, min((g + 1) * GROUP, OWNED)
@@ -73,10 +73,11 @@
         one = cot_ref[slot]
         cotl_ref[cells, :] = jnp.where(slot < count, one, jnp.zeros_like(one))
     cotl_ref[OWNED * OUT_PIX:, :] = jnp.zeros((OUT_PIX, C), BF)
-    cotp_ref[...] = jnp.dot(cotl_ref[...], perm_ref[...], preferred_element_type=F32).astype(BF)
     writes = []
     for g in range(STEPS):
         copies[g].wait()
+        patch_ref = first_ref if g == 0 else patch_s
+        base = 0 if g == 0 else (g - 1) * GROUP_ROWS
         for slot in range(g * GROUP, min((g + 1) * GROUP, OWNED)):
             off = [jnp.where(flags_ref[k, slot] > 0, 0.0, 1.0) for k in range(3)]
             for w, (first, size) in enumerate(WINDOWS):
@@ -86,28 +87,32 @@
                 chosen = (pick_ref[w] * keep)[:, :size]
                 got = jnp.dot(chosen, tiles_s[slot, first:first + size, :],
                               preferred_element_type=F32).astype(BF)
-                row = slot * ACT_PIX + 16 * w
+                row = base + (slot - g * GROUP) * ACT_PIX + 16 * w
                 for tap in range(TAPS):
                     patch_ref[row:row + 16, tap * C:(tap + 1) * C] = got[tap * 16:(tap + 1) * 16]
         if g == STEPS - 1:
-            patch_ref[OWNED * ACT_PIX:, :] = jnp.zeros((ACT_PIX, TAPS * C), BF)
+            patch_ref[REST_ROWS - ACT_PIX:, :] = jnp.zeros((ACT_PIX, TAPS * C), BF)
         rows = slice(g * GROUP_ROWS, (g + 1) * GROUP_ROWS)
         for tap in range(TAPS):
-            patcht_ref[tap * C:(tap + 1) * C, rows] = patch_ref[rows, tap * C:(tap + 1) * C].T
+            patcht_ref[tap * C:(tap + 1) * C, rows] = \
+                patch_ref[base:base + GROUP_ROWS, tap * C:(tap + 1) * C].T
         span = pl.ds(g * GROUP_ROWS, GROUP_ROWS)
-        writes.append(pltpu.make_async_copy(patch_ref.at[span, :], patch_hbm.at[span, :],
-                                            out_sems.at[2 * g]))
-        writes.append(pltpu.make_async_copy(patcht_ref.at[:, span], patcht_hbm.at[:, span],
-                                            out_sems.at[2 * g + 1]))
-        writes[2 * g].start()
-        writes[2 * g + 1].start()
+        started = [pltpu.make_async_copy(patcht_ref.at[:, span], patcht_hbm.at[:, span],
+                                         out_sems.at[2 * g])]
+        if g:
+            span = pl.ds(base, GROUP_ROWS)
+            started.append(pltpu.make_async_copy(patch_s.at[span, :], patch_hbm.at[span, :],
+                                                 out_sems.at[2 * g + 1]))
+        for write in started:
+            write.start()
+        writes += started
     for write in writes:
         write.wait()
 
 
-def fetch_kernel(patch_hbm, early_ref, sems):
-    spans = [pl.ds(r, 96) for r in range(0, EARLY_ROWS, 96)]
-    copies = [pltpu.make_async_copy(patch_hbm.at[span, :], early_ref.at[span, :], sems.at[k])
+def fetch_kernel(patch_hbm, rest_ref, sems):
+    spans = [pl.ds(r, 96) for r in range(0, REST_ROWS, 96)]
+    copies = [pltpu.make_async_copy(patch_hbm.at[span, :], rest_ref.at[span, :], sems.at[k])
               for k, span in enumerate(spans)]
     for copy in copies:
         copy.start()
@@ -120,23 +125,20 @@
         fetch_kernel,
         in_specs=[pl.BlockSpec(memory_space=pltpu.HBM)],
         out_specs=pl.BlockSpec(memory_space=pltpu.VMEM),
-        out_shape=jax.ShapeDtypeStruct((EARLY_ROWS, TAPS * C), BF),
-        scratch_shapes=[pltpu.SemaphoreType.DMA((EARLY_ROWS // 96,))],
+        out_shape=jax.ShapeDtypeStruct((REST_ROWS, TAPS * C), BF),
+        scratch_shapes=[pltpu.SemaphoreType.DMA((REST_ROWS // 96,))],
         compiler_params=pltpu.CompilerParams(vmem_limit_bytes=8 * 2**20),
         cost_estimate=pl.CostEstimate(flops=0, bytes_accessed=8 * 10**6, transcendentals=0),
         name="fetch",
     )(pltpu.with_memory_space_constraint(patches, pltpu.HBM))
 
 
-def main_kernel(core_ref, plan_ref, got_ref, other_ref, cotl_ref, cotp_ref, perm_ref, early_ref,
-                patch_hbm, patcht_hbm, feat_ref, keep_ref, send_ref,
-                late_s, patcht_s, spatial_s, temporal_s, pair_s, gpre_s, sems):
-    copies = [pltpu.make_async_copy(patch_hbm.at[pl.ds(EARLY_ROWS + r, 96), :],
-                                    late_s.at[pl.ds(r, 96), :], sems.at[r // 96])
-              for r in range(0, GROUP_ROWS, 96)]
-    copies += [pltpu.make_async_copy(patcht_hbm.at[pl.ds(tap * C, C), :],
-                                     patcht_s.at[pl.ds(tap * C, C), :], sems.at[4 + tap])
-               for tap in range(TAPS)]
+def main_kernel(core_ref, plan_ref, got_ref, other_ref, cotl_ref, perm_ref, first_ref, rest_ref,
+                patcht_hbm, feat_ref, keep_ref, send_ref,
+                patcht_s, spatial_s, temporal_s, pair_s, gpre_s, cotp_s, sems):
+    copies = [pltpu.make_async_copy(patcht_hbm.at[pl.ds(tap * C, C), :],
+                                    patcht_s.at[pl.ds(tap * C, C), :], sems.at[tap])
+              for tap in range(TAPS)]
     for copy in copies:
         copy.start()
     count = live_count(plan_ref)
@@ -156,11 +158,8 @@
         place(other_ref, got_ref)
 
     for g in range(STEPS):
-        if g == STEPS - 1:
-            for copy in copies:
-                copy.wait()
-        patch_ref = late_s if g == STEPS - 1 else early_ref
-        base = 0 if g == STEPS - 1 else g * GROUP_ROWS
+        patch_ref = rest_ref if g else first_ref
+        base = (g - 1) * GROUP_ROWS if g else 0
         rows = slice(g * GROUP_ROWS, (g + 1) * GROUP_ROWS)
         cells = slice(g * GROUP_COT, (g + 1) * GROUP_COT)
         pre = jnp.concatenate([
@@ -200,34 +199,37 @@
             keep_ref[b, lo - 144 * b:hi - 144 * b, :] = piece[:, :128]
             send_ref[b, lo - 144 * b:hi - 144 * b, :] = piece[:, 128:].astype(BF)
 
-    temporal = lax.dot_general(pair_s[...], cotp_ref[...], (((0,), (0,)), ((), ())),
+    cotp_s[...] = jnp.dot(cotl_ref[...], perm_ref[...], preferred_element_type=F32).astype(BF)
+    temporal = lax.dot_general(pair_s[...], cotp_s[...], (((0,), (0,)), ((), ())),
                                preferred_element_type=F32)
     for b in range(16):
         piece = temporal[b * 32:(b + 1) * 32]
         keep_ref[b, 144:, :] = piece[:, :128]
         send_ref[b, 144:, :] = piece[:, 128:].astype(BF)
+    for copy in copies:
+        copy.wait()
     for tap in range(TAPS):
         put(tap * C, jnp.dot(patcht_s[tap * C:(tap + 1) * C, :], gpre_s[...],
                              preferred_element_type=F32))
 
 
-def make_patches(flags, plan, tiles, cotangent, pick, marks, perm):
+def make_patches(flags, plan, tiles, cotangent, pick, marks):
     hbm = pl.BlockSpec(memory_space=pltpu.HBM)
     vmem = pl.BlockSpec(memory_space=pltpu.VMEM)
     smem = pl.BlockSpec(memory_space=pltpu.SMEM)
     return pl.pallas_call(
         patch_kernel,
-        in_specs=[smem, smem, hbm, vmem, vmem, vmem, vmem],
-        out_specs=[hbm, hbm, vmem, vmem],
+        in_specs=[smem, smem, hbm, vmem, vmem, vmem],
+        out_specs=[vmem, hbm, hbm, vmem],
         out_shape=[
-            pltpu.HBM((ROWS, TAPS * C), BF),
+            jax.ShapeDtypeStruct((GROUP_ROWS, TAPS * C), BF),
+            pltpu.HBM((REST_ROWS, TAPS * C), BF),
             pltpu.HBM((TAPS * C, ROWS), BF),
             jax.ShapeDtypeStruct((COT_ROWS, C), BF),
-            jax.ShapeDtypeStruct((COT_ROWS, C), BF),
         ],
         scratch_shapes=[
             pltpu.VMEM((OWNED, IN_PIX, C), BF),
-            pltpu.VMEM((ROWS, TAPS * C), BF),
+            pltpu.VMEM((REST_ROWS, TAPS * C), BF),
             pltpu.VMEM((TAPS * C, ROWS), BF),
             pltpu.SemaphoreType.DMA((STEPS,)),
             pltpu.SemaphoreType.DMA((2 * STEPS,)),
@@ -235,17 +237,16 @@
         compiler_params=pltpu.CompilerParams(vmem_limit_bytes=32 * 2**20),
         cost_estimate=pl.CostEstimate(flops=6 * 10**9, bytes_accessed=15 * 10**6, transcendentals=0),
         name="patches",
-    )(flags, plan, pltpu.with_memory_space_constraint(tiles, pltpu.HBM), cotangent, pick, marks,
-      perm)
-
-
-def run_section(core, plan, got, other, cot_live, cot_perm, perm, early, patches, patches_t):
+    )(flags, plan, pltpu.with_memory_space_constraint(tiles, pltpu.HBM), cotangent, pick, marks)
+
+
+def run_section(core, plan, got, other, cot_live, perm, first, rest, patches_t):
     hbm = pl.BlockSpec(memory_space=pltpu.HBM)
     vmem = pl.BlockSpec(memory_space=pltpu.VMEM)
     smem = pl.BlockSpec(memory_space=pltpu.SMEM)
     return pl.pallas_call(
         main_kernel,
-        in_specs=[smem] * 2 + [vmem] * 6 + [hbm] * 2,
+        in_specs=[smem] * 2 + [vmem] * 6 + [hbm],
         out_specs=[vmem] * 3,
         out_shape=[
             jax.ShapeDtypeStruct((OWNED, OUT_PIX, C), BF),
@@ -253,19 +254,18 @@
             jax.ShapeDtypeStruct((16, 176, 128), BF),
         ],
         scratch_shapes=[
-            pltpu.VMEM((GROUP_ROWS, TAPS * C), BF),
             pltpu.VMEM((TAPS * C, ROWS), BF),
             pltpu.VMEM((TAPS * C, C), BF),
             pltpu.VMEM((2 * C, C), BF),
             pltpu.VMEM((COT_ROWS, 2 * C), BF),
             pltpu.VMEM((ROWS, C), BF),
-            pltpu.SemaphoreType.DMA((4 + TAPS,)),
+            pltpu.VMEM((COT_ROWS, C), BF),
+            pltpu.SemaphoreType.DMA((TAPS,)),
         ],
         compiler_params=pltpu.CompilerParams(vmem_limit_bytes=36 * 2**20),
         cost_estimate=pl.CostEstimate(flops=4 * 10**9, bytes_accessed=15 * 10**6, transcendentals=0),
         name="section",
-    )(core, plan, got, other, cot_live, cot_perm, perm, early,
-      pltpu.with_memory_space_constraint(patches, pltpu.HBM),
+    )(core, plan, got, other, cot_live, perm, first, rest,
       pltpu.with_memory_space_constraint(patches_t, pltpu.HBM))
 
 
@@ -358,13 +358,13 @@
     perm = permutation(core)
     flags = halo_flags.T
     plan = send_plan[0].T
-    patches, patches_t, cot_live, cot_perm = make_patches(
-        flags, plan, tiles, cotangent, pick, marks, perm
+    first, patches, patches_t, cot_live = make_patches(
+        flags, plan, tiles, cotangent, pick, marks
     )
     got, patches, patches_t = lax.optimization_barrier((got, patches, patches_t))
     other = lax.ppermute(got, "dp", siblings)
     features, keep, send = run_section(
-        core_id, plan, got, other, cot_live, cot_perm, perm, fetch(patches), patches, patches_t
+        core_id, plan, got, other, cot_live, perm, first, fetch(patches), patches_t
     )
 
     theirs = lax.ppermute(send, "dp", siblings)

time: 85.7 us -> 85.4 us (level)
  Pallas kernels: 17.9 us -> 16.9 us
    pallas_call x2, Pallas kernels: 13.2 us -> 12.3 us  [the longest x1 6.49 us: make_patches(): pl.pallas_call(patch_kernel, in_specs=[smem, smem, hbm, vmem, vmem, vmem]...]
where the time goes in v4:
time: 85.4 us; the launch traced here: 85 us
  blocking collectives  45.7 us (54%)
  Pallas kernels  16.9 us (20%)
  starting transfers between devices  11.3 us (13%)
  waiting for transfers between devices  9.37 us (11%)
    all_to_all x1, blocking collectives, per_device(): last = lax.all_to_all(part, 'dp', 0, 0, axis_index_groups=along_z)  28.6 us
    all_to_all x1, blocking collectives, per_device(): part = lax.all_to_all(chip, 'bal', 0, 0)  17.1 us
    all_to_all x1, waiting for transfers between devices, per_device(): lax.all_to_all(spread(core_id, spatial_weight, temporal_weight), 'bal', 0...  7.46 us
    all_to_all x1, starting transfers between devices, per_device(): lax.all_to_all(spread(core_id, spatial_weight, temporal_weight), 'bal', 0...  7.05 us
    pallas_call x1, Pallas kernels, make_patches(): pl.pallas_call(patch_kernel, in_specs=[smem, smem, hbm, vmem, vmem, vmem]...  6.49 us
    pallas_call x1, Pallas kernels, run_section(): pl.pallas_call(main_kernel, in_specs=[smem] * 2 + [vmem] * 6 + [hbm], out...  5.8 us
    ppermute x1, starting transfers between devices, per_device(): theirs = lax.ppermute(send, 'dp', siblings)  2.31 us
    pallas_call x1, Pallas kernels, fetch(): pl.pallas_call(fetch_kernel, in_specs=[pl.BlockSpec(memory_space=pltpu.HB...  2.02 us
  transfers between devices with their start and end apart: 3, of which 3 were waited for; matrix products, arithmetic and copies ran while one was open for 1% of the time, Pallas kernels for 10%

profile of v4, /device:TPU:32, one launch (start us, length us, event | category | flops | bytes accessed | tf_op | source)
XLA Modules:
  0.0 85.0 jit_solution(8040542365519462289)
XLA Ops:
  0.6 0.0 copy-start.2
  0.6 0.0 copy-start.1
  0.7 0.0 copy-start
  0.7 1.9 %spread.1 = bf16[16,96,256]{2,1,0:T(8,128)(2,1)} custom-call(s32[1]{0:T(128)} %bitcast.core_ref, bf16[144,256]{1,0:T(8,128)(2,1)} %spatial_hbm.1, bf16[32,256]{1,0:T(8,128)(2,1)} %temporal_hbm.1), custom_call_target="tpu_custom_call" | custom-call | tf_op jit(solution)/shard_map/spread/pallas_call | solution.py:297
  2.6 7.0 %all-to-all-start = ((bf16[16,96,256]{2,1,0:T(8,128)(2,1)}), bf16[16,96,256]{2,1,0:T(8,128)(2,1)S(1)}, u32[]{:S(2)}, u32[]{:S(2)}) async-start(bf16[16,96,256]{2,1,0:T(8,128)(2,1)} %spread.1), calls=%async_computation | async-start | bytes 1572864 | tf_op jit(solution)/shard_map/all_to_all | solution.py:355
  9.7 0.3 fusion.35.pick_ref
  10.1 0.1 fusion.49.mark_ref
  10.2 0.0 copy-done.2
  10.2 0.0 copy-done.1
  10.2 0.0 copy-done
  10.2 6.5 %patches.1 = (bf16[384,2304]{1,0:T(8,128)(2,1)S(1)}, bf16[768,2304]{1,0:T(8,128)(2,1)}, bf16[2304,1152]{1,0:T(8,128)(2,1)}, bf16[768,256]{1,0:T(8,128)(2,1)S(1)}) custom-call(s32[3,23]{1,0:T(4,128)S(1)} %bitcast.9, s32[2,16]{1,0:T(2,128)S(1)} %bitcast.10, bf16[23,270,256]{2,1,0:T(8,128)(2,1)} %tiles_hbm.1, bf16[23,32,256]{2,1,0:T(8,128)(2,1)S(1)} %copy-done, ...), custom_call_target="tpu_custom_call" | custom-call | flops 6000000000 | bytes 15000000 | tf_op jit(solution)/shard_map/patches/pallas_call | solution.py:220
  16.7 7.5 %all-to-all-done.got_ref = bf16[16,96,256]{2,1,0:T(8,128)(2,1)S(1)} async-done(((bf16[16,96,256]{2,1,0:T(8,128)(2,1)}), bf16[16,96,256]{2,1,0:T(8,128)(2,1)S(1)}, u32[]{:S(2)}, u32[]{:S(2)}) %all-to-all-start) | async-done | bytes 786464 | tf_op jit(solution)/shard_map/all_to_all | solution.py:355
  24.2 1.9 %collective-permute-start = (bf16[16,96,256]{2,1,0:T(8,128)(2,1)S(1)}, bf16[16,96,256]{2,1,0:T(8,128)(2,1)S(1)}, u32[]{:S(2)}, u32[]{:S(2)}) collective-permute-start(bf16[16,96,256]{2,1,0:T(8,128)(2,1)S(1)} %all-to-all-done.got_ref), channel_id=1, source_target_pairs={{0,16},{16,0},{32,48},{48,32},{64,80},{80,64},{96,112},{112,96},{1... | collective-permute-start | bytes 2359304 | tf_op jit(solution)/shard_map/ppermute | solution.py:365
  26.2 2.0 %fetch.1.rest_ref = bf16[768,2304]{1,0:T(8,128)(2,1)S(1)} custom-call(bf16[768,2304]{1,0:T(8,128)(2,1)} %get-tuple-element.20.patch_hbm), custom_call_target="tpu_custom_call" | custom-call | bytes 8000000 | tf_op jit(solution)/shard_map/fetch/pallas_call | solution.py:124
  28.2 0.1 collective-permute-done.other_ref
  28.3 5.8 %section.1 = (bf16[23,32,256]{2,1,0:T(8,128)(2,1)}, f32[16,176,128]{2,1,0:T(8,128)S(1)}, bf16[16,176,128]{2,1,0:T(8,128)(2,1)S(1)}) custom-call(s32[1]{0:T(128)} %bitcast.core_ref, s32[2,16]{1,0:T(2,128)S(1)} %bitcast.11, bf16[16,96,256]{2,1,0:T(8,128)(2,1)S(1)} %all-to-all-done.got_ref, bf16[16,96,256]{2,1,0:T(8,128)(2,1)S(1)} %collective-permute-done.other_ref, ...), custom_call_target="tpu_custom_call" | custom-call | flops 4000000000 | bytes 15000000 | tf_op jit(solution)/shard_map/section/pallas_call | solution.py:247
  34.1 2.3 %collective-permute-start.1 = (bf16[16,176,128]{2,1,0:T(8,128)(2,1)S(1)}, bf16[16,176,128]{2,1,0:T(8,128)(2,1)S(1)}, u32[]{:S(2)}, u32[]{:S(2)}) collective-permute-start(bf16[16,176,128]{2,1,0:T(8,128)(2,1)S(1)} %get-tuple-element.24), channel_id=1, source_target_pairs={{0,16},{16,0},{32,48},{48,32},{64,80},{80,64},{96,112},{112,96},{1... | collective-permute-start | bytes 2162696 | tf_op jit(solution)/shard_map/ppermute | solution.py:370
  36.5 1.8 %collective-permute-done.1 = bf16[16,176,128]{2,1,0:T(8,128)(2,1)S(1)} collective-permute-done((bf16[16,176,128]{2,1,0:T(8,128)(2,1)S(1)}, bf16[16,176,128]{2,1,0:T(8,128)(2,1)S(1)}, u32[]{:S(2)}, u32[]{:S(2)}) %collective-permute-start.1) | collective-permute-done | bytes 720928 | tf_op jit(solution)/shard_map/ppermute | solution.py:370
  38.3 0.2 add_convert_fusion
  38.4 17.1 %all_to_all.15 = bf16[16,176,128]{2,1,0:T(8,128)(2,1)S(1)} all-to-all(bf16[16,176,128]{2,1,0:T(8,128)(2,1)S(1)} %add_convert_fusion), channel_id=1, replica_groups=mesh['dp'=32,'bal'=16] {'bal'}, dimensions={0} | all-to-all | bytes 1441792 | tf_op jit(solution)/shard_map/all_to_all | solution.py:372
  55.5 0.1 convert_reduce_fusion
  55.6 0.1 copy.9
  55.7 28.6 %all_to_all.16.part_ref = f32[16,8,176]{2,1,0:T(8,128)S(1)} all-to-all(f32[16,8,176]{2,1,0:T(8,128)S(1)} %bitcast.12), channel_id=1, replica_groups={{0,32,64,96,128,160,192,224,256,288,320,352,384,416,448,480},{16,48,80,..., dimensions={0} | all-to-all | bytes 180224 | tf_op jit(solution)/shard_map/all_to_all | solution.py:376
  84.3 0.7 finish.1
  (12 shorter events, 0.1 us)
Async XLA Ops:
  0.6 9.6 %copy-start.2 = (s32[1,16,2]{1,2,0:T(2,128)S(1)}, s32[1,16,2]{1,2,0:T(2,128)}, u32[]{:S(2)}) copy-start(s32[1,16,2]{1,2,0:T(2,128)} %param.9) | copy-start | bytes 388
  0.6 9.6 %copy-start.1 = (s32[23,3]{0,1:T(4,128)S(1)}, s32[23,3]{0,1:T(4,128)}, u32[]{:S(2)}) copy-start(s32[23,3]{0,1:T(4,128)} %param.8) | copy-start | bytes 832
  0.7 9.6 %copy-start = (bf16[23,32,256]{2,1,0:T(8,128)(2,1)S(1)}, bf16[23,32,256]{2,1,0:T(8,128)(2,1)}, u32[]{:S(2)}) copy-start(bf16[23,32,256]{2,1,0:T(8,128)(2,1)} %cot_ref.1) | copy-start | bytes 1130500
  2.6 21.6 %all-to-all-start = ((bf16[16,96,256]{2,1,0:T(8,128)(2,1)}), bf16[16,96,256]{2,1,0:T(8,128)(2,1)S(1)}, u32[]{:S(2)}, u32[]{:S(2)}) async-start(bf16[16,96,256]{2,1,0:T(8,128)(2,1)} %spread.1), calls=%async_computation | async-start | bytes 1572864 | tf_op jit(solution)/shard_map/all_to_all | solution.py:355
  24.2 4.2 %collective-permute-start = (bf16[16,96,256]{2,1,0:T(8,128)(2,1)S(1)}, bf16[16,96,256]{2,1,0:T(8,128)(2,1)S(1)}, u32[]{:S(2)}, u32[]{:S(2)}) collective-permute-start(bf16[16,96,256]{2,1,0:T(8,128)(2,1)S(1)} %all-to-all-done.got_ref), channel_id=1, source_target_pairs={{0,16},{16,0},{32,48},{48,32},{64,80},{80,64},{96,112},{112,96},{1... | collective-permute-start | bytes 2359304 | tf_op jit(solution)/shard_map/ppermute | solution.py:365
  34.1 4.1 %collective-permute-start.1 = (bf16[16,176,128]{2,1,0:T(8,128)(2,1)S(1)}, bf16[16,176,128]{2,1,0:T(8,128)(2,1)S(1)}, u32[]{:S(2)}, u32[]{:S(2)}) collective-permute-start(bf16[16,176,128]{2,1,0:T(8,128)(2,1)S(1)} %get-tuple-element.24), channel_id=1, source_target_pairs={{0,16},{16,0},{32,48},{48,32},{64,80},{80,64},{96,112},{112,96},{1... | collective-permute-start | bytes 2162696 | tf_op jit(solution)/shard_map/ppermute | solution.py:370

commit v5 on v4

--- a/solution.py
+++ b/solution.py
@@ -110,32 +110,35 @@
         write.wait()
 
 
-def fetch_kernel(patch_hbm, rest_ref, sems):
-    spans = [pl.ds(r, 96) for r in range(0, REST_ROWS, 96)]
-    copies = [pltpu.make_async_copy(patch_hbm.at[span, :], rest_ref.at[span, :], sems.at[k])
-              for k, span in enumerate(spans)]
+def fetch_kernel(first_ref, patch_hbm, all_ref, sems):
+    copies = [pltpu.make_async_copy(patch_hbm.at[pl.ds(r, 96), :],
+                                    all_ref.at[pl.ds(GROUP_ROWS + r, 96), :], sems.at[r // 96])
+              for r in range(0, REST_ROWS, 96)]
+    copies += [pltpu.make_async_copy(first_ref.at[pl.ds(r, 96), :], all_ref.at[pl.ds(r, 96), :],
+                                     sems.at[(REST_ROWS + r) // 96])
+               for r in range(0, GROUP_ROWS, 96)]
     for copy in copies:
         copy.start()
     for copy in copies:
         copy.wait()
 
 
-def fetch(patches):
+def fetch(first, patches):
     return pl.pallas_call(
         fetch_kernel,
-        in_specs=[pl.BlockSpec(memory_space=pltpu.HBM)],
+        in_specs=[pl.BlockSpec(memory_space=pltpu.VMEM), pl.BlockSpec(memory_space=pltpu.HBM)],
         out_specs=pl.BlockSpec(memory_space=pltpu.VMEM),
-        out_shape=jax.ShapeDtypeStruct((REST_ROWS, TAPS * C), BF),
-        scratch_shapes=[pltpu.SemaphoreType.DMA((REST_ROWS // 96,))],
+        out_shape=jax.ShapeDtypeStruct((ROWS, TAPS * C), BF),
+        scratch_shapes=[pltpu.SemaphoreType.DMA((ROWS // 96,))],
         compiler_params=pltpu.CompilerParams(vmem_limit_bytes=8 * 2**20),
         cost_estimate=pl.CostEstimate(flops=0, bytes_accessed=8 * 10**6, transcendentals=0),
         name="fetch",
-    )(pltpu.with_memory_space_constraint(patches, pltpu.HBM))
-
-
-def main_kernel(core_ref, plan_ref, got_ref, other_ref, cotl_ref, perm_ref, first_ref, rest_ref,
-                patcht_hbm, feat_ref, keep_ref, send_ref,
-                patcht_s, spatial_s, temporal_s, pair_s, gpre_s, cotp_s, sems):
+    )(first, pltpu.with_memory_space_constraint(patches, pltpu.HBM))
+
+
+def main_kernel(core_ref, plan_ref, got_ref, other_ref, cotl_ref, perm_ref, patch_ref,
+                patcht_hbm, feat_hbm, keep_ref, send_ref,
+                feat_s, patcht_s, spatial_s, temporal_s, pair_s, gpre_s, cotp_s, sems):
     copies = [pltpu.make_async_copy(patcht_hbm.at[pl.ds(tap * C, C), :],
                                     patcht_s.at[pl.ds(tap * C, C), :], sems.at[tap])
               for tap in range(TAPS)]
@@ -157,39 +160,32 @@
     def _():
         place(other_ref, got_ref)
 
-    for g in range(STEPS):
-        patch_ref = rest_ref if g else first_ref
-        base = (g - 1) * GROUP_ROWS if g else 0
-        rows = slice(g * GROUP_ROWS, (g + 1) * GROUP_ROWS)
-        cells = slice(g * GROUP_COT, (g + 1) * GROUP_COT)
-        pre = jnp.concatenate([
-            jnp.dot(patch_ref[r:r + DOT_ROWS, :], spatial_s[...], preferred_element_type=F32)
-            for r in range(base, base + GROUP_ROWS, DOT_ROWS)
-        ], axis=0)
-        sig = 1.0 / (1.0 + jnp.exp(-pre))
-        act = (pre * sig).astype(BF)
-        slope = sig * (1.0 + pre * (1.0 - sig))
-        for t in range(GROUP):
-            out = slice(g * GROUP_COT + t * OUT_PIX, g * GROUP_COT + (t + 1) * OUT_PIX)
-            pair_s[out, :C] = act[t * ACT_PIX + 16:(t + 1) * ACT_PIX]
-            pair_s[out, C:] = act[t * ACT_PIX:t * ACT_PIX + OUT_PIX]
-        gpair = lax.dot_general(cotl_ref[cells, :], temporal_s[...], (((1,), (1,)), ((), ())),
-                                preferred_element_type=F32)
-        pieces = []
-        for t in range(GROUP):
-            a, b, c = t * OUT_PIX, t * OUT_PIX + 16, (t + 1) * OUT_PIX
-            pieces.append(gpair[a:b, C:])
-            pieces.append(gpair[a:b, :C] + gpair[b:c, C:])
-            pieces.append(gpair[b:c, :C])
-        gact = jnp.concatenate(pieces, axis=0)
-        gpre = (gact * slope).astype(BF)
-        gpre_s[rows, :] = jnp.dot(gpre, perm_ref[...], preferred_element_type=F32).astype(BF)
-        feat = jnp.dot(pair_s[cells, :], temporal_s[...], preferred_element_type=F32).astype(BF)
-        for t in range(GROUP):
-            slot = g * GROUP + t
-            if slot < OWNED:
-                one = feat[t * OUT_PIX:(t + 1) * OUT_PIX]
-                feat_ref[slot] = jnp.where(slot < count, one, jnp.zeros_like(one))
+    pre = jnp.concatenate([
+        jnp.dot(patch_ref[r:r + DOT_ROWS, :], spatial_s[...], preferred_element_type=F32)
+        for r in range(0, ROWS, DOT_ROWS)
+    ], axis=0)
+    sig = 1.0 / (1.0 + jnp.exp(-pre))
+    act = (pre * sig).astype(BF)
+    slope = sig * (1.0 + pre * (1.0 - sig))
+    gpair = lax.dot_general(cotl_ref[...], temporal_s[...], (((1,), (1,)), ((), ())),
+                            preferred_element_type=F32)
+    pieces = []
+    for t in range(PAD_TILES):
+        cells = slice(t * OUT_PIX, (t + 1) * OUT_PIX)
+        pair_s[cells, :C] = act[t * ACT_PIX + 16:(t + 1) * ACT_PIX]
+        pair_s[cells, C:] = act[t * ACT_PIX:t * ACT_PIX + OUT_PIX]
+        a, b, c = t * OUT_PIX, t * OUT_PIX + 16, (t + 1) * OUT_PIX
+        pieces.append(gpair[a:b, C:])
+        pieces.append(gpair[a:b, :C] + gpair[b:c, C:])
+        pieces.append(gpair[b:c, :C])
+    gpre = (jnp.concatenate(pieces, axis=0) * slope).astype(BF)
+    gpre_s[...] = jnp.dot(gpre, perm_ref[...], preferred_element_type=F32).astype(BF)
+    feat = jnp.dot(pair_s[...], temporal_s[...], preferred_element_type=F32).astype(BF)
+    for slot in range(OWNED):
+        one = feat[slot * OUT_PIX:(slot + 1) * OUT_PIX]
+        feat_s[slot] = jnp.where(slot < count, one, jnp.zeros_like(one))
+    output = pltpu.make_async_copy(feat_s, feat_hbm, sems.at[TAPS])
+    output.start()
 
     def put(first, grad):
         last = first + grad.shape[0]
@@ -211,6 +207,7 @@
     for tap in range(TAPS):
         put(tap * C, jnp.dot(patcht_s[tap * C:(tap + 1) * C, :], gpre_s[...],
                              preferred_element_type=F32))
+    output.wait()
 
 
 def make_patches(flags, plan, tiles, cotangent, pick, marks):
@@ -240,32 +237,33 @@
     )(flags, plan, pltpu.with_memory_space_constraint(tiles, pltpu.HBM), cotangent, pick, marks)
 
 
-def run_section(core, plan, got, other, cot_live, perm, first, rest, patches_t):
+def run_section(core, plan, got, other, cot_live, perm, patches, patches_t):
     hbm = pl.BlockSpec(memory_space=pltpu.HBM)
     vmem = pl.BlockSpec(memory_space=pltpu.VMEM)
     smem = pl.BlockSpec(memory_space=pltpu.SMEM)
     return pl.pallas_call(
         main_kernel,
-        in_specs=[smem] * 2 + [vmem] * 6 + [hbm],
-        out_specs=[vmem] * 3,
+        in_specs=[smem] * 2 + [vmem] * 5 + [hbm],
+        out_specs=[hbm, vmem, vmem],
         out_shape=[
-            jax.ShapeDtypeStruct((OWNED, OUT_PIX, C), BF),
+            pltpu.HBM((OWNED, OUT_PIX, C), BF),
             jax.ShapeDtypeStruct((16, 176, 128), F32),
             jax.ShapeDtypeStruct((16, 176, 128), BF),
         ],
         scratch_shapes=[
+            pltpu.VMEM((OWNED, OUT_PIX, C), BF),
             pltpu.VMEM((TAPS * C, ROWS), BF),
             pltpu.VMEM((TAPS * C, C), BF),
             pltpu.VMEM((2 * C, C), BF),
             pltpu.VMEM((COT_ROWS, 2 * C), BF),
             pltpu.VMEM((ROWS, C), BF),
             pltpu.VMEM((COT_ROWS, C), BF),
-            pltpu.SemaphoreType.DMA((TAPS,)),
+            pltpu.SemaphoreType.DMA((TAPS + 1,)),
         ],
         compiler_params=pltpu.CompilerParams(vmem_limit_bytes=36 * 2**20),
         cost_estimate=pl.CostEstimate(flops=4 * 10**9, bytes_accessed=15 * 10**6, transcendentals=0),
         name="section",
-    )(core, plan, got, other, cot_live, perm, first, rest,
+    )(core, plan, got, other, cot_live, perm, patches,
       pltpu.with_memory_space_constraint(patches_t, pltpu.HBM))
 
 
@@ -364,7 +362,7 @@
     got, patches, patches_t = lax.optimization_barrier((got, patches, patches_t))
     other = lax.ppermute(got, "dp", siblings)
     features, keep, send = run_section(
-        core_id, plan, got, other, cot_live, perm, first, fetch(patches), patches_t
+        core_id, plan, got, other, cot_live, perm, fetch(first, patches), patches_t
     )
 
     theirs = lax.ppermute(send, "dp", siblings)

time: 85.4 us -> 85 us (level)
  no operation moved by 1% of the time
where the time goes in v5:
time: 85 us; the launch traced here: 84.6 us
  blocking collectives  45.7 us (54%)
  Pallas kernels  16.5 us (19%)
  starting transfers between devices  11.3 us (13%)
  waiting for transfers between devices  9.33 us (11%)
  between operations  0.85 us (1%)
    all_to_all x1, blocking collectives, per_device(): last = lax.all_to_all(part, 'dp', 0, 0, axis_index_groups=along_z)  28.6 us
    all_to_all x1, blocking collectives, per_device(): part = lax.all_to_all(chip, 'bal', 0, 0)  17.1 us
    all_to_all x1, waiting for transfers between devices, per_device(): lax.all_to_all(spread(core_id, spatial_weight, temporal_weight), 'bal', 0...  7.46 us
    all_to_all x1, starting transfers between devices, per_device(): lax.all_to_all(spread(core_id, spatial_weight, temporal_weight), 'bal', 0...  7.05 us
    pallas_call x1, Pallas kernels, make_patches(): pl.pallas_call(patch_kernel, in_specs=[smem, smem, hbm, vmem, vmem, vmem]...  6.48 us
    pallas_call x1, Pallas kernels, run_section(): pl.pallas_call(main_kernel, in_specs=[smem] * 2 + [vmem] * 5 + [hbm], out...  5.37 us
    ppermute x1, starting transfers between devices, per_device(): theirs = lax.ppermute(send, 'dp', siblings)  2.36 us
    pallas_call x1, Pallas kernels, fetch(): pl.pallas_call(fetch_kernel, in_specs=[pl.BlockSpec(memory_space=pltpu.VM...  2.06 us
  transfers between devices with their start and end apart: 3, of which 3 were waited for; matrix products, arithmetic and copies ran while one was open for 1% of the time, Pallas kernels for 10%

profile of v5, /device:TPU:32, one launch (start us, length us, event | category | flops | bytes accessed | tf_op | source)
XLA Modules:
  0.0 84.6 jit_solution(4165580726690988377)
XLA Ops:
  0.6 0.0 copy-start.2
  0.6 0.0 copy-start.1
  0.7 0.0 copy-start
  0.7 1.9 %spread.1 = bf16[16,96,256]{2,1,0:T(8,128)(2,1)} custom-call(s32[1]{0:T(128)} %bitcast.core_ref, bf16[144,256]{1,0:T(8,128)(2,1)} %spatial_hbm.1, bf16[32,256]{1,0:T(8,128)(2,1)} %temporal_hbm.1), custom_call_target="tpu_custom_call" | custom-call | tf_op jit(solution)/shard_map/spread/pallas_call | solution.py:295
  2.6 7.0 %all-to-all-start = ((bf16[16,96,256]{2,1,0:T(8,128)(2,1)}), bf16[16,96,256]{2,1,0:T(8,128)(2,1)S(1)}, u32[]{:S(2)}, u32[]{:S(2)}) async-start(bf16[16,96,256]{2,1,0:T(8,128)(2,1)} %spread.1), calls=%async_computation | async-start | bytes 1572864 | tf_op jit(solution)/shard_map/all_to_all | solution.py:353
  9.7 0.3 fusion.35.pick_ref
  10.1 0.1 fusion.49.mark_ref
  10.2 0.0 copy-done.2
  10.2 0.0 copy-done.1
  10.2 0.0 copy-done
  10.2 6.5 %patches.1 = (bf16[384,2304]{1,0:T(8,128)(2,1)S(1)}, bf16[768,2304]{1,0:T(8,128)(2,1)}, bf16[2304,1152]{1,0:T(8,128)(2,1)}, bf16[768,256]{1,0:T(8,128)(2,1)S(1)}) custom-call(s32[3,23]{1,0:T(4,128)S(1)} %bitcast.9, s32[2,16]{1,0:T(2,128)S(1)} %bitcast.10, bf16[23,270,256]{2,1,0:T(8,128)(2,1)} %tiles_hbm.1, bf16[23,32,256]{2,1,0:T(8,128)(2,1)S(1)} %copy-done, ...), custom_call_target="tpu_custom_call" | custom-call | flops 6000000000 | bytes 15000000 | tf_op jit(solution)/shard_map/patches/pallas_call | solution.py:217
  16.7 7.5 %all-to-all-done.got_ref = bf16[16,96,256]{2,1,0:T(8,128)(2,1)S(1)} async-done(((bf16[16,96,256]{2,1,0:T(8,128)(2,1)}), bf16[16,96,256]{2,1,0:T(8,128)(2,1)S(1)}, u32[]{:S(2)}, u32[]{:S(2)}) %all-to-all-start) | async-done | bytes 786464 | tf_op jit(solution)/shard_map/all_to_all | solution.py:353
  24.2 1.9 %collective-permute-start = (bf16[16,96,256]{2,1,0:T(8,128)(2,1)S(1)}, bf16[16,96,256]{2,1,0:T(8,128)(2,1)S(1)}, u32[]{:S(2)}, u32[]{:S(2)}) collective-permute-start(bf16[16,96,256]{2,1,0:T(8,128)(2,1)S(1)} %all-to-all-done.got_ref), channel_id=1, source_target_pairs={{0,16},{16,0},{32,48},{48,32},{64,80},{80,64},{96,112},{112,96},{1... | collective-permute-start | bytes 2359304 | tf_op jit(solution)/shard_map/ppermute | solution.py:363
  26.2 2.1 %fetch.1.patch_ref = bf16[1152,2304]{1,0:T(8,128)(2,1)S(1)} custom-call(bf16[384,2304]{1,0:T(8,128)(2,1)S(1)} %get-tuple-element.19.first_ref, bf16[768,2304]{1,0:T(8,128)(2,1)} %get-tuple-element.20.patch_hbm), custom_call_target="tpu_custom_call" | custom-call | bytes 8000000 | tf_op jit(solution)/shard_map/fetch/pallas_call | solution.py:127
  28.3 0.1 collective-permute-done.other_ref
  28.3 5.4 %section.1 = (bf16[23,32,256]{2,1,0:T(8,128)(2,1)}, f32[16,176,128]{2,1,0:T(8,128)S(1)}, bf16[16,176,128]{2,1,0:T(8,128)(2,1)S(1)}) custom-call(s32[1]{0:T(128)} %bitcast.core_ref, s32[2,16]{1,0:T(2,128)S(1)} %bitcast.11, bf16[16,96,256]{2,1,0:T(8,128)(2,1)S(1)} %all-to-all-done.got_ref, bf16[16,96,256]{2,1,0:T(8,128)(2,1)S(1)} %collective-permute-done.other_ref, ...), custom_call_target="tpu_custom_call" | custom-call | flops 4000000000 | bytes 15000000 | tf_op jit(solution)/shard_map/section/pallas_call | solution.py:244
  33.7 2.4 %collective-permute-start.1 = (bf16[16,176,128]{2,1,0:T(8,128)(2,1)S(1)}, bf16[16,176,128]{2,1,0:T(8,128)(2,1)S(1)}, u32[]{:S(2)}, u32[]{:S(2)}) collective-permute-start(bf16[16,176,128]{2,1,0:T(8,128)(2,1)S(1)} %get-tuple-element.24), channel_id=1, source_target_pairs={{0,16},{16,0},{32,48},{48,32},{64,80},{80,64},{96,112},{112,96},{1... | collective-permute-start | bytes 2162696 | tf_op jit(solution)/shard_map/ppermute | solution.py:368
  36.1 1.8 %collective-permute-done.1 = bf16[16,176,128]{2,1,0:T(8,128)(2,1)S(1)} collective-permute-done((bf16[16,176,128]{2,1,0:T(8,128)(2,1)S(1)}, bf16[16,176,128]{2,1,0:T(8,128)(2,1)S(1)}, u32[]{:S(2)}, u32[]{:S(2)}) %collective-permute-start.1) | collective-permute-done | bytes 720928 | tf_op jit(solution)/shard_map/ppermute | solution.py:368
  37.9 0.2 add_convert_fusion
  38.0 17.1 %all_to_all.15 = bf16[16,176,128]{2,1,0:T(8,128)(2,1)S(1)} all-to-all(bf16[16,176,128]{2,1,0:T(8,128)(2,1)S(1)} %add_convert_fusion), channel_id=1, replica_groups=mesh['dp'=32,'bal'=16] {'bal'}, dimensions={0} | all-to-all | bytes 1441792 | tf_op jit(solution)/shard_map/all_to_all | solution.py:370
  55.1 0.1 convert_reduce_fusion
  55.2 0.1 copy.9
  55.3 28.6 %all_to_all.16.part_ref = f32[16,8,176]{2,1,0:T(8,128)S(1)} all-to-all(f32[16,8,176]{2,1,0:T(8,128)S(1)} %bitcast.12), channel_id=1, replica_groups={{0,32,64,96,128,160,192,224,256,288,320,352,384,416,448,480},{16,48,80,..., dimensions={0} | all-to-all | bytes 180224 | tf_op jit(solution)/shard_map/all_to_all | solution.py:374
  83.9 0.7 finish.1
  (12 shorter events, 0.1 us)
Async XLA Ops:
  0.6 9.6 %copy-start.2 = (s32[1,16,2]{1,2,0:T(2,128)S(1)}, s32[1,16,2]{1,2,0:T(2,128)}, u32[]{:S(2)}) copy-start(s32[1,16,2]{1,2,0:T(2,128)} %param.9) | copy-start | bytes 388
  0.6 9.6 %copy-start.1 = (s32[23,3]{0,1:T(4,128)S(1)}, s32[23,3]{0,1:T(4,128)}, u32[]{:S(2)}) copy-start(s32[23,3]{0,1:T(4,128)} %param.8) | copy-start | bytes 832
  0.7 9.6 %copy-start = (bf16[23,32,256]{2,1,0:T(8,128)(2,1)S(1)}, bf16[23,32,256]{2,1,0:T(8,128)(2,1)}, u32[]{:S(2)}) copy-start(bf16[23,32,256]{2,1,0:T(8,128)(2,1)} %cot_ref.1) | copy-start | bytes 1130500
  2.6 21.6 %all-to-all-start = ((bf16[16,96,256]{2,1,0:T(8,128)(2,1)}), bf16[16,96,256]{2,1,0:T(8,128)(2,1)S(1)}, u32[]{:S(2)}, u32[]{:S(2)}) async-start(bf16[16,96,256]{2,1,0:T(8,128)(2,1)} %spread.1), calls=%async_computation | async-start | bytes 1572864 | tf_op jit(solution)/shard_map/all_to_all | solution.py:353
  24.2 4.2 %collective-permute-start = (bf16[16,96,256]{2,1,0:T(8,128)(2,1)S(1)}, bf16[16,96,256]{2,1,0:T(8,128)(2,1)S(1)}, u32[]{:S(2)}, u32[]{:S(2)}) collective-permute-start(bf16[16,96,256]{2,1,0:T(8,128)(2,1)S(1)} %all-to-all-done.got_ref), channel_id=1, source_target_pairs={{0,16},{16,0},{32,48},{48,32},{64,80},{80,64},{96,112},{112,96},{1... | collective-permute-start | bytes 2359304 | tf_op jit(solution)/shard_map/ppermute | solution.py:363
  33.7 4.2 %collective-permute-start.1 = (bf16[16,176,128]{2,1,0:T(8,128)(2,1)S(1)}, bf16[16,176,128]{2,1,0:T(8,128)(2,1)S(1)}, u32[]{:S(2)}, u32[]{:S(2)}) collective-permute-start(bf16[16,176,128]{2,1,0:T(8,128)(2,1)S(1)} %get-tuple-element.24), channel_id=1, source_target_pairs={{0,16},{16,0},{32,48},{48,32},{64,80},{80,64},{96,112},{112,96},{1... | collective-permute-start | bytes 2162696 | tf_op jit(solution)/shard_map/ppermute | solution.py:368
